TPU v7x, 512 devices: a whole 4x8x8 slice. The times are simulated.
512 devices in a mesh: replica: 64 (over x, y, core), section: 8 (over z).
Axes of the slice: x: 4, y: 8, z: 8, core: 2. Of those that a mesh axis runs over, the one named last changes fastest.
Arguments:
- gradients: bfloat16 [64, 512, 5120], P('replica', 'section')
- momentum: float32 [64, 512, 5120], P('replica', 'section'), may hold values from -12 to 12
- keep_block: int32 [64, 8, 80], P('replica', 'section'), may hold values from 0 to 63
Outputs:
- new_momentum: float32 [64, 512, 5120], P('replica', 'section')
- update: bfloat16 [512, 5120], P('section')
All inputs are finite; a program needn't handle non-finite values.
Results may differ from a plain program's by a relative error of at most 0.0028.
Values may be sent and summed in bfloat16 or wider, within the bound.
A program may use at most 128 MiB of HBM per device.

v0:
```python
import jax
import jax.numpy as jnp
from jax import lax
from jax.sharding import PartitionSpec as P

GROUP = 64
BLOCK = 8


momentum_decay = 0.9
epsilon = 1e-06


def dct_basis():
    freq_index = jnp.arange(GROUP, dtype=jnp.float32)[:, None]
    cell_index = jnp.arange(GROUP, dtype=jnp.float32)[None, :]
    table = jnp.sqrt(2.0 / GROUP) * jnp.cos(
        jnp.pi * (2.0 * cell_index + 1.0) * freq_index / (2.0 * GROUP)
    )
    first_row = jnp.where(jnp.arange(GROUP) == 0, 1.0 / jnp.sqrt(2.0), 1.0)
    return table * first_row[:, None]


def inverse_blocks(basis, dense, row_blocks, col_blocks):
    return jnp.einsum(
        "ki,rkcl,lj->ricj",
        basis,
        dense.reshape(row_blocks, GROUP, col_blocks, GROUP),
        basis,
        precision=lax.Precision.HIGHEST,
    )


def per_device(gradients, momentum, keep_block):
    high = lax.Precision.HIGHEST
    basis = dct_basis()
    per_side = GROUP // BLOCK
    moments = momentum_decay * momentum[0] + gradients[0].astype(jnp.float32)
    local_rows = moments.shape[0]
    width = moments.shape[1]
    row_blocks = local_rows // GROUP
    col_blocks = width // GROUP
    tile_grid = moments.reshape(row_blocks, GROUP, col_blocks, GROUP)
    spectrum = jnp.einsum("ki,ricj,lj->rkcl", basis, tile_grid, basis, precision=high)
    spectrum = spectrum.reshape(row_blocks, per_side, BLOCK, col_blocks, per_side, BLOCK)
    block_range = jnp.arange(per_side * per_side, dtype=jnp.int32)
    selector = (keep_block[0][..., None] == block_range).astype(jnp.float32)
    selector = selector.reshape(row_blocks, col_blocks, per_side, per_side)
    kept_vals = jnp.einsum("rcyx,ryicxj->rcij", selector, spectrum, precision=high)
    own_dense = jnp.einsum("rcyx,rcij->ryicxj", selector, kept_vals, precision=high)
    own_space = inverse_blocks(basis, own_dense, row_blocks, col_blocks).reshape(local_rows, width)
    new_moments = moments - own_space
    entry_count = float(local_rows * lax.axis_size("section") * width)
    my_share = lax.psum_scatter(own_space, "replica", scatter_dimension=1, tiled=True)
    squares = lax.psum(jnp.sum(my_share * my_share), ("replica", "section"))
    scaled = (my_share * lax.rsqrt(squares / entry_count + epsilon)).astype(jnp.bfloat16)
    update = lax.all_gather(scaled, "replica", axis=1, tiled=True)
    return (new_moments[None], update)


def solution(mesh):
    placed = (
        P("replica", "section", None),
        P("replica", "section", None),
        P("replica", "section", None),
    )
    return jax.shard_map(
        per_device,
        mesh=mesh,
        in_specs=placed,
        out_specs=(P("replica", "section", None), P("section", None)),
        check_vma=False,
    )
```

profile of v0, /device:TPU:1, one launch (start us, length us, event | category | flops | bytes accessed | tf_op | source)
XLA Modules:
  0.0 346.6 jit_solution(16880807143354517132)
XLA Ops:
  7.2 0.0 reduce-scatter.4.cloned.1.call-start
  7.2 1.7 convert_add_fusion
  8.9 2.2 add.39
  11.1 3.2 copy.18
  14.4 2.2 fusion.12
  16.5 0.0 copy-start
  16.6 3.5 fusion.4
  20.0 0.0 copy-done
  20.0 0.1 fusion.14
  20.1 0.2 multiply_reduce_fusion
  20.3 0.2 broadcast_multiply_fusion
  20.6 3.4 fusion.2
  24.0 3.6 %fusion.6 = f32[1,64,80,64]{2,3,1,0:T(8,128)S(1)} fusion(f32[80,64,64]{0,2,1:T(8,128)S(1)} %fusion.2, f32[64]{0:T(128)S(1)} %get-tuple-element.4, f32[64]{0:T(128)S(1)} %get-tuple-element.5), kind=kOutput, calls=%fused_computation.7 | convolution fusion | flops 251670528 | bytes 2621952 | tf_op jit(solution)/shard_map/ki,rkcl,lj->ricj/dot_general | solution.py:25
  27.7 3.4 copy.39
  31.0 0.0 reduce-scatter.4.cloned.1.call-update
  31.1 2.1 copy.24
  33.2 2.2 reshape.94
  35.4 146.0 %reduce-scatter.4.cloned.1.call-done = f32[80,64]{1,0:T(8,128)} async-done(((f32[5120,64]{1,0:T(8,128)}), f32[80,64]{1,0:T(8,128)}) %reduce-scatter.4.cloned.1.call-update) | async-done | bytes 20496
  181.4 0.8 copy.38
  182.3 0.6 multiply_reduce_fusion.1
  182.9 1.2 sub.4
  184.1 101.7 %psum.7 = f32[]{:T(128)} all-reduce(f32[]{:T(128)} %multiply_reduce_fusion.1), channel_id=1, replica_groups=mesh['replica'=64,'section'=8] {'replica','section'}, use_global_device_ids=true, to_apply=%region_2.3 | all-reduce | flops 1 | bytes 8 | tf_op jit(solution)/shard_map/psum | solution.py:55
  286.5 49.7 %all-gather = bf16[64,80,64]{1,2,0:T(8,128)(2,1)S(1)} all-gather(bf16[1,80,64]{1,2,0:T(8,128)(2,1)S(1)} %fusion.15), channel_id=1, replica_groups=mesh['replica'=64,'section'=8] {'replica'}, dimensions={0}, use_global_device_ids=true | all-gather | bytes 665600 | tf_op jit(solution)/shard_map/all_gather | solution.py:57
  336.1 0.7 copy.26
  336.8 2.9 reshape.97
  (3 shorter events, 0.0 us)
Async XLA Ops:
  7.2 174.3 %reduce-scatter.4.cloned.1.call-start = ((), (), s32[]{:S(2)}) async-start(), calls=%async_computation.1 | async-start | bytes 2662400
  16.5 3.5 %copy-start = (s32[1,1,80]{2,1,0:T(1,128)S(1)}, s32[1,1,80]{2,1,0:T(1,128)}, u32[]{:S(2)}) copy-start(s32[1,1,80]{2,1,0:T(1,128)} %param.5) | copy-start | bytes 964
Sparse Core Ops, SparseCore 0:
  31.2 150.2 reduce-scatter.3
where the time goes:
time: 347 us
  blocking collectives  151 us (44%)
  waiting for transfers between devices  146 us (42%)
  local copies, waits for them, and re-layouts  17.6 us (5%)
  between operations  14.8 us (4%)
  matrix products  12.7 us (4%)
  other arithmetic  4.04 us (1%)
    unnamed x2, waiting for transfers between devices  146 us
    psum x1, blocking collectives, per_device(): squares = lax.psum(jnp.sum(my_share * my_share), ('replica', 'section'))  102 us
    all_gather x1, blocking collectives, per_device(): update = lax.all_gather(scaled, 'replica', axis=1, tiled=True)  49.7 us
    unnamed x5, local copies, waits for them, and re-layouts  7.16 us
    dot_general x2, matrix products, inverse_blocks(): jnp.einsum('ki,rkcl,lj->ricj', basis, dense.reshape(row_blocks, GROUP, co...  7.05 us
  transfers between devices with their start and end apart: 1, of which 1 were waited for; matrix products, arithmetic and copies ran while one was open for 1% of the time, Pallas kernels for 0%

commit v1 on v0

v1 whole, which is shorter than its diff:
```python
import functools

import jax
import jax.numpy as jnp
import ml_dtypes
import numpy as np
from jax import lax
from jax.experimental import pallas as pl
from jax.experimental.pallas import tpu as pltpu
from jax.sharding import PartitionSpec as P

GROUP = 64
BLOCK = 8
SIDE = GROUP // BLOCK
LANES = 128
CHIPS_X, CHIPS_Y, CORES = 4, 8, 2
OWNERS = CHIPS_X * CORES
MESH = pl.DeviceIdType.MESH
F32, BF16 = jnp.float32, jnp.bfloat16

momentum_decay = 0.9
epsilon = 1e-06


def dct_basis():
    k = np.arange(GROUP, dtype=np.float64)[:, None]
    n = np.arange(GROUP, dtype=np.float64)[None, :]
    basis = np.sqrt(2.0 / GROUP) * np.cos(np.pi * (2.0 * n + 1.0) * k / (2.0 * GROUP))
    basis[0] /= np.sqrt(2.0)
    return basis.astype(np.float32)


def two_terms(values):
    high = values.astype(ml_dtypes.bfloat16)
    low = (values - high.astype(np.float32)).astype(ml_dtypes.bfloat16)
    return high, low


def constant_tables():
    basis = dct_basis()

    def right(matrix):
        high, low = two_terms(np.kron(np.eye(2, dtype=np.float32), matrix))
        return np.concatenate([high, high, low], axis=0)

    def left(matrix):
        high, low = two_terms(matrix)
        wide = np.concatenate([high, high, low, np.zeros_like(low)], axis=1)
        return np.concatenate([wide[:, :LANES], wide[:, LANES:]], axis=0)

    return np.concatenate([right(basis.T), right(basis), left(basis), left(basis.T)], axis=0)


def split(values):
    high = values.astype(BF16)
    low = (values - high.astype(F32)).astype(BF16)
    return high, low


def mm(a, b):
    return jnp.dot(a, b, preferred_element_type=F32)


def kernel(
    entry_count, pairs, kb_ref, g_ref, m_ref, tab_ref, nm_ref, upd_ref,
    g_buf, x_buf, tab, masked, fold, spread, compact, tiles_x, tiles_y, sums_x, sums_z, upd,
    g_sem, m_sem, tab_sem, nm_sem, out_sem,
    x_send, x_recv, y_send, y_recv, sx_send, sx_recv, sz_send, sz_recv, f_send, f_recv, c_send, c_recv,
):
    width = pairs * LANES
    n_blocks = 2 * pairs
    replica, section = lax.axis_index("replica"), lax.axis_index("section")
    x = replica // (CHIPS_Y * CORES)
    y = (replica // CORES) % CHIPS_Y
    core = replica % CORES
    mine = x * CORES + core

    def peer(dx=0, dy=0, dc=0, dz=0):
        px, py, pc = (x + dx) % CHIPS_X, (y + dy) % CHIPS_Y, (core + dc) % CORES
        return ((px * CHIPS_Y + py) * CORES + pc, (section + dz) % 8)

    group_x = [(dx, dc) for dx in range(CHIPS_X) for dc in range(CORES)][1:]

    loads = []
    tab_load = pltpu.make_async_copy(tab_ref, tab, tab_sem)
    for s in range(OWNERS):
        cols = slice(s * width, (s + 1) * width)
        pair = (
            pltpu.make_async_copy(m_ref.at[:, cols], x_buf.at[:, cols], m_sem.at[s]),
            pltpu.make_async_copy(g_ref.at[:, cols], g_buf.at[:, cols], g_sem.at[s]),
        )
        loads.append(pair)
        pair[0].start()
        pair[1].start()
        if s == 0:
            tab_load.start()

    barrier = pltpu.get_barrier_semaphore()
    everyone = (
        [peer(dx=dx, dc=dc) for dx, dc in group_x]
        + [peer(dy=d) for d in range(1, CHIPS_Y)]
        + [peer(dz=d) for d in range(1, 8)]
    )
    for other in everyone:
        pl.semaphore_signal(barrier, inc=1, device_id=other, device_id_type=MESH)

    lane8 = lax.broadcasted_iota(jnp.int32, (BLOCK, LANES), 1)
    upper = lane8 >= GROUP
    lane_q = (lane8 % GROUP) // BLOCK
    row_f = lax.broadcasted_iota(jnp.int32, (width, LANES), 0)
    lane_f = lax.broadcasted_iota(jnp.int32, (width, LANES), 1)
    fold[...] = jnp.where((row_f // GROUP) * BLOCK + row_f % BLOCK == lane_f, 1.0, 0.0).astype(BF16)
    row_t = lax.broadcasted_iota(jnp.int32, (LANES, width), 0)
    lane_t = lax.broadcasted_iota(jnp.int32, (LANES, width), 1)
    block_t = lane_t // GROUP
    spread[:, 0:width] = jnp.where(row_t == block_t * BLOCK + lane_t % BLOCK, 1.0, 0.0).astype(BF16)
    spread[:, width : 2 * width] = jnp.where(row_t == BLOCK * n_blocks + block_t, 1.0, 0.0).astype(BF16)
    spread[:, 2 * width : 3 * width] = jnp.where(row_t == (BLOCK + 1) * n_blocks + block_t, 1.0, 0.0).astype(BF16)

    tab_load.wait()
    right_fwd = tab[0:384, :]
    right_inv = tab[384:768, :]
    left_fwd = jnp.concatenate([tab[768:832, :], tab[832:896, 0:64]], axis=1)
    left_inv = jnp.concatenate([tab[896:960, :], tab[960:1024, 0:64]], axis=1)

    def block_rows(s, j):
        c = s * n_blocks + 2 * j
        return kb_ref[0, c], kb_ref[0, c + 1]

    def p_lanes(s, j):
        k0, k1 = block_rows(s, j)
        return jnp.where(upper, k1 // SIDE, k0 // SIDE)

    def q_lanes(s, j):
        k0, k1 = block_rows(s, j)
        return jnp.where(upper, k1 % SIDE, k0 % SIDE)

    for s in range(OWNERS):
        cols = slice(s * width, (s + 1) * width)
        loads[s][0].wait()
        loads[s][1].wait()
        moments = momentum_decay * x_buf[:, cols] + g_buf[:, cols].astype(F32)
        x_buf[:, cols] = moments
        high, low = split(moments)
        rows = mm(left_fwd, jnp.concatenate([high, low, high], axis=0))
        chosen = []
        for j in range(pairs):
            p_of = p_lanes(s, j)
            picked = jnp.zeros((BLOCK, LANES), F32)
            for p in range(SIDE):
                picked = jnp.where(p_of == p, rows[p * BLOCK : (p + 1) * BLOCK, j * LANES : (j + 1) * LANES], picked)
            chosen.append(picked)
        high, low = split(jnp.concatenate(chosen, axis=0))
        spectrum = mm(jnp.concatenate([high, low, high], axis=1), right_fwd)
        for j in range(pairs):
            kept = jnp.where(q_lanes(s, j) == lane_q, spectrum[j * BLOCK : (j + 1) * BLOCK, :], 0.0)
            masked[s * BLOCK : (s + 1) * BLOCK, j * LANES : (j + 1) * LANES] = kept

    high, low = split(masked[...])
    packed = mm(high, fold[...]) + mm(low, fold[...])
    for s in range(OWNERS):
        tile = packed[s * BLOCK : (s + 1) * BLOCK, :]
        for b in range(n_blocks):
            k = kb_ref[0, s * n_blocks + b]
            tile = jnp.where(lane8 == BLOCK * n_blocks + b, (k // SIDE).astype(F32), tile)
            tile = jnp.where(lane8 == (BLOCK + 1) * n_blocks + b, (k % SIDE).astype(F32), tile)
        compact[s] = tile

    pl.semaphore_wait(barrier, len(everyone))

    sends_x = []
    for i, (dx, dc) in enumerate(group_x, start=1):
        px, pc = (x + dx) % CHIPS_X, (core + dc) % CORES
        copy = pltpu.make_async_remote_copy(
            src_ref=compact.at[px * CORES + pc], dst_ref=tiles_x.at[i], send_sem=x_send.at[i], recv_sem=x_recv.at[i],
            device_id=peer(dx=dx, dc=dc), device_id_type=MESH,
        )
        copy.start()
        sends_x.append(copy)
    tiles_x[0] = compact[mine]

    stores = []

    def own_part(s):
        cols = slice(s * width, (s + 1) * width)
        stacked = jnp.concatenate(
            [masked[s * BLOCK : (s + 1) * BLOCK, j * LANES : (j + 1) * LANES] for j in range(pairs)], axis=0
        )
        high, low = split(stacked)
        wide = mm(jnp.concatenate([high, low, high], axis=1), right_inv)
        placed = []
        for j in range(pairs):
            p_of = p_lanes(s, j)
            piece = wide[j * BLOCK : (j + 1) * BLOCK, :]
            placed.append(jnp.concatenate([jnp.where(p_of == p, piece, 0.0) for p in range(SIDE)], axis=0))
        high, low = split(jnp.concatenate(placed, axis=1))
        own = mm(left_inv, jnp.concatenate([high, low, high], axis=0))
        x_buf[:, cols] = x_buf[:, cols] - own
        copy = pltpu.make_async_copy(x_buf.at[:, cols], nm_ref.at[:, cols], nm_sem.at[s])
        copy.start()
        stores.append(copy)

    for s in range(0, 3):
        own_part(s)

    for copy in sends_x:
        copy.wait_recv()

    tiles_y[0] = tiles_x[...]
    sends_y = []
    for d in range(1, CHIPS_Y):
        copy = pltpu.make_async_remote_copy(
            src_ref=tiles_x, dst_ref=tiles_y.at[d], send_sem=y_send.at[d], recv_sem=y_recv.at[d],
            device_id=peer(dy=d), device_id_type=MESH,
        )
        copy.start()
        sends_y.append(copy)

    for s in range(3, OWNERS):
        own_part(s)

    for copy in sends_y:
        copy.wait_recv()

    n_rows = CHIPS_Y * OWNERS * BLOCK
    received = tiles_y[...].reshape(n_rows, LANES)
    high, low = split(received)
    lane_r = lax.broadcasted_iota(jnp.int32, (n_rows, LANES), 1) % GROUP
    row_r = lax.broadcasted_iota(jnp.int32, (n_rows, LANES), 0) % BLOCK
    group_r = (lane_r // BLOCK).astype(F32)
    same_row = (lane_r % BLOCK) == row_r
    total_spectrum = []
    for j in range(pairs):
        part = slice(j * LANES, (j + 1) * LANES)
        values = mm(high, spread[:, part]) + mm(low, spread[:, part])
        p_of = mm(high, spread[:, width + j * LANES : width + (j + 1) * LANES])
        q_of = mm(high, spread[:, 2 * width + j * LANES : 2 * width + (j + 1) * LANES])
        values = jnp.where(q_of == group_r, values, 0.0)
        place = jnp.where(same_row & (p_of == group_r), 1.0, 0.0).astype(BF16)
        v_high, v_low = split(values)
        dims = (((0,), (0,)), ((), ()))
        both = lax.dot_general(place, v_high, dims, preferred_element_type=F32) + lax.dot_general(
            place, v_low, dims, preferred_element_type=F32
        )
        lane64 = lax.broadcasted_iota(jnp.int32, (GROUP, LANES), 1)
        total_spectrum.append(jnp.where(lane64 >= GROUP, both[GROUP:, :], both[:GROUP, :]))

    squares = jnp.zeros((BLOCK, LANES), F32)
    for part in total_spectrum:
        for p in range(SIDE):
            piece = part[p * BLOCK : (p + 1) * BLOCK, :]
            squares = squares + piece * piece
    sums_x[0] = squares
    sends_sx = []
    for i, (dx, dc) in enumerate(group_x, start=1):
        copy = pltpu.make_async_remote_copy(
            src_ref=sums_x.at[0], dst_ref=sums_x.at[i], send_sem=sx_send.at[i], recv_sem=sx_recv.at[i],
            device_id=peer(dx=dx, dc=dc), device_id_type=MESH,
        )
        copy.start()
        sends_sx.append(copy)

    high, low = split(jnp.concatenate(total_spectrum, axis=0))
    wide = mm(jnp.concatenate([high, low, high], axis=1), right_inv)
    high, low = split(jnp.concatenate([wide[j * GROUP : (j + 1) * GROUP, :] for j in range(pairs)], axis=1))
    total = mm(left_inv, jnp.concatenate([high, low, high], axis=0))

    for copy in sends_sx:
        copy.wait_recv()
    sums_z[0] = jnp.sum(sums_x[...], axis=0)
    sends_sz = []
    for d in range(1, 8):
        copy = pltpu.make_async_remote_copy(
            src_ref=sums_z.at[0], dst_ref=sums_z.at[d], send_sem=sz_send.at[d], recv_sem=sz_recv.at[d],
            device_id=peer(dz=d), device_id_type=MESH,
        )
        copy.start()
        sends_sz.append(copy)
    for copy in sends_sz:
        copy.wait_recv()
    everything = jnp.sum(sums_z[...], axis=0)
    square_sum = jnp.sum(jnp.sum(everything, axis=0, keepdims=True), axis=1, keepdims=True)
    scale = lax.rsqrt(square_sum / entry_count + epsilon)
    upd[mine] = (total * scale).astype(BF16)

    def to_core(slot, i):
        return pltpu.make_async_remote_copy(
            src_ref=upd.at[slot], dst_ref=upd.at[slot], send_sem=c_send.at[i], recv_sem=c_recv.at[i],
            device_id=peer(dc=1), device_id_type=MESH,
        )

    def to_out(slot, i):
        return pltpu.make_async_copy(
            upd.at[slot], upd_ref.at[:, pl.ds(pl.multiple_of(slot * width, LANES), width)], out_sem.at[i]
        )

    sends_f, sends_c, outs = [], [], []
    for d in (1, 3, 2):
        copy = pltpu.make_async_remote_copy(
            src_ref=upd.at[mine], dst_ref=upd.at[mine], send_sem=f_send.at[d], recv_sem=f_recv.at[d],
            device_id=peer(dx=d), device_id_type=MESH,
        )
        copy.start()
        sends_f.append(copy)
    copy = to_core(mine, 0)
    copy.start()
    sends_c.append(copy)
    copy = to_out(mine, 0)
    copy.start()
    outs.append(copy)
    for d in (1, 3, 2):
        slot = ((x + CHIPS_X - d) % CHIPS_X) * CORES + core
        pltpu.make_async_remote_copy(
            src_ref=upd.at[slot], dst_ref=upd.at[slot], send_sem=f_send.at[d], recv_sem=f_recv.at[d],
            device_id=peer(dx=d), device_id_type=MESH,
        ).wait_recv()
        copy = to_core(slot, d)
        copy.start()
        sends_c.append(copy)
        copy = to_out(slot, d)
        copy.start()
        outs.append(copy)
    for i, d in enumerate((0, 1, 3, 2)):
        slot = ((x + CHIPS_X - d) % CHIPS_X) * CORES + (core + 1) % CORES
        pltpu.make_async_remote_copy(
            src_ref=upd.at[slot], dst_ref=upd.at[slot], send_sem=c_send.at[d], recv_sem=c_recv.at[d],
            device_id=peer(dc=1), device_id_type=MESH,
        ).wait_recv()
        copy = to_out(slot, 4 + i)
        copy.start()
        outs.append(copy)

    for copy in sends_x + sends_y + sends_sx + sends_sz + sends_f + sends_c:
        copy.wait_send()
    for copy in stores + outs:
        copy.wait()


def per_device(gradients, momentum, keep_block):
    local_rows, columns = gradients.shape[1:]
    pairs = columns // (OWNERS * LANES)
    width = pairs * LANES
    tables = jnp.asarray(constant_tables())
    entry_count = float(local_rows * lax.axis_size("section") * columns)
    dma = pltpu.SemaphoreType.DMA
    new_momentum, update = pl.pallas_call(
        functools.partial(kernel, entry_count, pairs),
        out_shape=(
            jax.ShapeDtypeStruct((local_rows, columns), F32),
            jax.ShapeDtypeStruct((local_rows, columns), BF16),
        ),
        in_specs=[pl.BlockSpec(memory_space=pltpu.SMEM)] + [pl.BlockSpec(memory_space=pl.ANY)] * 3,
        out_specs=(pl.BlockSpec(memory_space=pl.ANY), pl.BlockSpec(memory_space=pl.ANY)),
        scratch_shapes=[
            pltpu.VMEM((local_rows, columns), BF16),
            pltpu.VMEM((local_rows, columns), F32),
            pltpu.VMEM(tables.shape, BF16),
            pltpu.VMEM((OWNERS * BLOCK, width), F32),
            pltpu.VMEM((width, LANES), BF16),
            pltpu.VMEM((LANES, 3 * width), BF16),
            pltpu.VMEM((OWNERS, BLOCK, LANES), F32),
            pltpu.VMEM((OWNERS, BLOCK, LANES), F32),
            pltpu.VMEM((CHIPS_Y, OWNERS, BLOCK, LANES), F32),
            pltpu.VMEM((OWNERS, BLOCK, LANES), F32),
            pltpu.VMEM((8, BLOCK, LANES), F32),
            pltpu.VMEM((OWNERS, local_rows, width), BF16),
            dma((OWNERS,)), dma((OWNERS,)), dma, dma((OWNERS,)), dma((OWNERS,)),
            dma((OWNERS,)), dma((OWNERS,)), dma((CHIPS_Y,)), dma((CHIPS_Y,)),
            dma((OWNERS,)), dma((OWNERS,)), dma((8,)), dma((8,)),
            dma((CHIPS_X,)), dma((CHIPS_X,)), dma((CHIPS_X,)), dma((CHIPS_X,)),
        ],
        compiler_params=pltpu.CompilerParams(collective_id=0, has_side_effects=True, vmem_limit_bytes=60 << 20),
        name="kept_blocks_step",
    )(keep_block[0], gradients[0], momentum[0], tables)
    return new_momentum[None], update


def solution(mesh):
    placed = (
        P("replica", "section", None),
        P("replica", "section", None),
        P("replica", "section", None),
    )
    return jax.shard_map(
        per_device,
        mesh=mesh,
        in_specs=placed,
        out_specs=(P("replica", "section", None), P("section", None)),
        check_vma=False,
    )
```

time: 347 us -> 53.2 us (0.15)
  blocking collectives: 151 us -> 0 us
  waiting for transfers between devices: 146 us -> 0 us
  Pallas kernels: 0 us -> 49 us
  local copies, waits for them, and re-layouts: 17.6 us -> 3.37 us
  between operations: 14.8 us -> 0.65 us
  matrix products: 12.7 us -> 0 us
  other arithmetic: 4.04 us -> 0 us
    unnamed x2 -> x0, waiting for transfers between devices: 146 us -> none
    psum x1 -> x0, blocking collectives: 102 us -> none  [per_device(): squares = lax.psum(jnp.sum(my_share * my_share), ('replica', 'section'))]
    all_gather x1 -> x0, blocking collectives: 49.7 us -> none  [per_device(): update = lax.all_gather(scaled, 'replica', axis=1, tiled=True)]
    pallas_call x0 -> x1, Pallas kernels: none -> 49 us  [per_device(): pl.pallas_call(functools.partial(kernel, entry_count, pairs), out_shape=(...]
    dot_general x4 -> x0, matrix products: 12.7 us -> none  [the longest x2 7.05 us: inverse_blocks(): jnp.einsum('ki,rkcl,lj->ricj', basis, dense.reshape(row_blocks, GROUP, co...]
    add x2 -> x0, local copies, waits for them, and re-layouts: 5.45 us -> none  [per_device(): moments = momentum_decay * momentum[0] + gradients[0].astype(jnp.float32)]
    unnamed x5 -> x4, local copies, waits for them, and re-layouts: 7.16 us -> 3.37 us
  transfers between devices with their start and end apart: 1 -> 0, of which waited for: 1 -> 0; matrix products, arithmetic and copies ran while one was open for 1% -> 0% of each run, Pallas kernels for 0% -> 0%
where the time goes in v1:
time: 53.2 us; the launch traced here: 53 us
  Pallas kernels  49 us (92%)
  local copies, waits for them, and re-layouts  3.37 us (6%)
  between operations  0.65 us (1%)
    pallas_call x1, Pallas kernels, per_device(): pl.pallas_call(functools.partial(kernel, entry_count, pairs), out_shape=(...  49 us
    unnamed x4, local copies, waits for them, and re-layouts  3.37 us

profile of v1, /device:TPU:1, one launch (start us, length us, event | category | flops | bytes accessed | tf_op | source)
XLA Modules:
  0.0 53.0 jit_solution(471639159914374349)
XLA Ops:
  0.6 49.0 %kept_blocks_step.1 = (f32[64,5120]{1,0:T(8,128)}, bf16[64,5120]{1,0:T(8,128)(2,1)}) custom-call(s32[1,80]{1,0:T(1,128)} %bitcast.7, bf16[64,5120]{1,0:T(8,128)(2,1)} %bitcast.6, f32[64,5120]{1,0:T(8,128)} %bitcast.4, bf16[1024,128]{1,0:T(8,128)(2,1)} %constant.2.clone.tab_ref), custom_call_target="tpu_custom_call" | custom-call | tf_op jit(solution)/shard_map/kept_blocks_step/pallas_call | solution.py:346
  49.6 0.0 copy-start
  49.7 2.5 %copy.8 = f32[1,64,5120]{2,1,0:T(8,128)} copy(f32[1,64,5120]{2,1,0:T(8,128)} %bitcast.5) | data formatting | bytes 2621440
  52.2 0.0 copy-done
  52.2 0.8 %copy.9 = bf16[64,5120]{1,0:T(8,128)(2,1)} copy(bf16[64,5120]{1,0:T(8,128)(2,1)S(1)} %copy-done) | data formatting | bytes 1310720
Async XLA Ops:
  49.6 2.5 %copy-start = (bf16[64,5120]{1,0:T(8,128)(2,1)S(1)}, bf16[64,5120]{1,0:T(8,128)(2,1)}, u32[]{:S(2)}) copy-start(bf16[64,5120]{1,0:T(8,128)(2,1)} %get-tuple-element.9) | copy-start | bytes 1966084

commit v2 on v1

v2 whole, which is shorter than its diff:
```python
import functools

import jax
import jax.numpy as jnp
import ml_dtypes
import numpy as np
from jax import lax
from jax.experimental import pallas as pl
from jax.experimental.pallas import tpu as pltpu
from jax.sharding import PartitionSpec as P

GROUP = 64
BLOCK = 8
SIDE = GROUP // BLOCK
LANES = 128
CHIPS_X, CHIPS_Y, CORES, SECTIONS = 4, 8, 2, 8
OWNERS = CHIPS_X * CORES
MESH = pl.DeviceIdType.MESH
F32, BF16 = jnp.float32, jnp.bfloat16

momentum_decay = 0.9
epsilon = 1e-06


def dct_basis():
    k = np.arange(GROUP, dtype=np.float64)[:, None]
    n = np.arange(GROUP, dtype=np.float64)[None, :]
    basis = np.sqrt(2.0 / GROUP) * np.cos(np.pi * (2.0 * n + 1.0) * k / (2.0 * GROUP))
    basis[0] /= np.sqrt(2.0)
    return basis.astype(np.float32)


def two_terms(values):
    high = values.astype(ml_dtypes.bfloat16)
    low = (values - high.astype(np.float32)).astype(ml_dtypes.bfloat16)
    return high, low


def constant_tables():
    basis = dct_basis()

    def right(matrix):
        high, low = two_terms(np.kron(np.eye(2, dtype=np.float32), matrix))
        return np.concatenate([high, high, low], axis=0)

    def left(matrix):
        high, low = two_terms(matrix)
        wide = np.concatenate([high, high, low, np.zeros_like(low)], axis=1)
        return np.concatenate([wide[:, :LANES], wide[:, LANES:]], axis=0)

    return np.concatenate([right(basis.T), right(basis), left(basis), left(basis.T)], axis=0)


def split(values):
    high = values.astype(BF16)
    low = (values - high.astype(F32)).astype(BF16)
    return high, low


def mm(a, b):
    return jnp.dot(a, b, preferred_element_type=F32)


def kernel(
    pairs, kb_hbm, g_ref, m_ref, tab_ref, nm_ref, total_ref, sums_ref,
    kb_ref, g_buf, m_buf, tab, masked, fold, spread, compact, tiles_x, tiles_y, sums_x,
    load_sem, kb_sem, send_sem, recv_sem, gather_send, gather_recv,
):
    width = pairs * LANES
    n_blocks = 2 * pairs
    replica, section = lax.axis_index("replica"), lax.axis_index("section")
    x = replica // (CHIPS_Y * CORES)
    y = (replica // CORES) % CHIPS_Y
    core = replica % CORES
    mine = x * CORES + core

    def peer(dx=0, dy=0, dc=0, dz=0):
        px, py, pc = (x + dx) % CHIPS_X, (y + dy) % CHIPS_Y, (core + dc) % CORES
        return ((px * CHIPS_Y + py) * CORES + pc, (section + dz) % SECTIONS)

    group_x = [(dx, dc) for dx in range(CHIPS_X) for dc in range(CORES)][1:]

    half = OWNERS // 2 * width
    loads = []
    kb_load = pltpu.make_async_copy(kb_hbm, kb_ref, kb_sem)
    tab_load = pltpu.make_async_copy(tab_ref, tab, load_sem.at[4])
    for h in range(2):
        cols = slice(h * half, (h + 1) * half)
        pair = (
            pltpu.make_async_copy(m_ref.at[:, cols], m_buf.at[:, cols], load_sem.at[2 * h]),
            pltpu.make_async_copy(g_ref.at[:, cols], g_buf.at[:, cols], load_sem.at[2 * h + 1]),
        )
        loads.append(pair)
        pair[0].start()
        pair[1].start()
        if h == 0:
            kb_load.start()
            tab_load.start()

    barrier = pltpu.get_barrier_semaphore()
    everyone = (
        [peer(dx=dx, dc=dc) for dx, dc in group_x]
        + [peer(dy=d) for d in range(1, CHIPS_Y)]
        + [peer(dz=d) for d in range(1, SECTIONS)]
    )
    for other in everyone:
        pl.semaphore_signal(barrier, inc=1, device_id=other, device_id_type=MESH)

    lane8 = lax.broadcasted_iota(jnp.int32, (BLOCK, LANES), 1)
    upper = lane8 >= GROUP
    lane_q = (lane8 % GROUP) // BLOCK
    row_f = lax.broadcasted_iota(jnp.int32, (width, LANES), 0)
    lane_f = lax.broadcasted_iota(jnp.int32, (width, LANES), 1)
    fold[...] = jnp.where((row_f // GROUP) * BLOCK + row_f % BLOCK == lane_f, 1.0, 0.0).astype(BF16)
    row_t = lax.broadcasted_iota(jnp.int32, (LANES, width), 0)
    lane_t = lax.broadcasted_iota(jnp.int32, (LANES, width), 1)
    block_t = lane_t // GROUP
    spread[:, 0:width] = jnp.where(row_t == block_t * BLOCK + lane_t % BLOCK, 1.0, 0.0).astype(BF16)
    spread[:, width : 2 * width] = jnp.where(row_t == BLOCK * n_blocks + block_t, 1.0, 0.0).astype(BF16)
    spread[:, 2 * width : 3 * width] = jnp.where(row_t == (BLOCK + 1) * n_blocks + block_t, 1.0, 0.0).astype(BF16)

    kb_load.wait()
    tab_load.wait()
    right_fwd = tab[0:384, :]
    right_inv = tab[384:768, :]
    left_fwd = jnp.concatenate([tab[768:832, :], tab[832:896, 0:64]], axis=1)
    left_inv = jnp.concatenate([tab[896:960, :], tab[960:1024, 0:64]], axis=1)

    def block_pair(s, j):
        c = s * n_blocks + 2 * j
        return kb_ref[0, c], kb_ref[0, c + 1]

    def p_lanes(s, j):
        k0, k1 = block_pair(s, j)
        return jnp.where(upper, k1 // SIDE, k0 // SIDE)

    def q_lanes(s, j):
        k0, k1 = block_pair(s, j)
        return jnp.where(upper, k1 % SIDE, k0 % SIDE)

    chosen = []
    for s in range(OWNERS):
        if s % (OWNERS // 2) == 0:
            for copy in loads[s // (OWNERS // 2)]:
                copy.wait()
        cols = slice(s * width, (s + 1) * width)
        moments = momentum_decay * m_buf[:, cols] + g_buf[:, cols].astype(F32)
        nm_ref[:, cols] = moments
        high, low = split(moments)
        rows = mm(left_fwd, jnp.concatenate([high, low, high], axis=0))
        for j in range(pairs):
            p_of = p_lanes(s, j)
            picked = jnp.zeros((BLOCK, LANES), F32)
            for p in range(SIDE):
                picked = jnp.where(p_of == p, rows[p * BLOCK : (p + 1) * BLOCK, j * LANES : (j + 1) * LANES], picked)
            chosen.append(picked)

    high, low = split(jnp.concatenate(chosen, axis=0))
    spectrum = mm(jnp.concatenate([high, low, high], axis=1), right_fwd)
    for s in range(OWNERS):
        for j in range(pairs):
            row = (s * pairs + j) * BLOCK
            kept = jnp.where(q_lanes(s, j) == lane_q, spectrum[row : row + BLOCK, :], 0.0)
            masked[s * BLOCK : (s + 1) * BLOCK, j * LANES : (j + 1) * LANES] = kept

    high, low = split(masked[...])
    packed = mm(high, fold[...]) + mm(low, fold[...])
    for s in range(OWNERS):
        tile = packed[s * BLOCK : (s + 1) * BLOCK, :]
        for b in range(n_blocks):
            k = kb_ref[0, s * n_blocks + b]
            tile = jnp.where(lane8 == BLOCK * n_blocks + b, (k // SIDE).astype(F32), tile)
            tile = jnp.where(lane8 == (BLOCK + 1) * n_blocks + b, (k % SIDE).astype(F32), tile)
        compact[s] = tile

    pl.semaphore_wait(barrier, len(everyone))

    def send(src, dst, i, other):
        copy = pltpu.make_async_remote_copy(
            src_ref=src, dst_ref=dst, send_sem=send_sem.at[i], recv_sem=recv_sem.at[i],
            device_id=other, device_id_type=MESH,
        )
        copy.start()

    def all_of(ref, i):
        return pltpu.make_async_remote_copy(
            src_ref=ref, dst_ref=ref, send_sem=send_sem.at[i], recv_sem=recv_sem.at[i],
            device_id=peer(dc=1), device_id_type=MESH,
        )

    for i, (dx, dc) in enumerate(group_x, start=1):
        px, pc = (x + dx) % CHIPS_X, (core + dc) % CORES
        send(compact.at[px * CORES + pc], tiles_x.at[i], 0, peer(dx=dx, dc=dc))
    tiles_x[0] = compact[mine]

    wide = []
    for s in range(OWNERS):
        stacked = jnp.concatenate(
            [masked[s * BLOCK : (s + 1) * BLOCK, j * LANES : (j + 1) * LANES] for j in range(pairs)], axis=0
        )
        wide.append(stacked)
    high, low = split(jnp.concatenate(wide, axis=0))
    wide = mm(jnp.concatenate([high, low, high], axis=1), right_inv)
    for s in range(OWNERS):
        cols = slice(s * width, (s + 1) * width)
        placed = []
        for j in range(pairs):
            p_of = p_lanes(s, j)
            row = (s * pairs + j) * BLOCK
            piece = wide[row : row + BLOCK, :]
            placed.append(jnp.concatenate([jnp.where(p_of == p, piece, 0.0) for p in range(SIDE)], axis=0))
        high, low = split(jnp.concatenate(placed, axis=1))
        nm_ref[:, cols] = nm_ref[:, cols] - mm(left_inv, jnp.concatenate([high, low, high], axis=0))

    all_of(tiles_x.at[1:OWNERS], 0).wait_recv()

    tiles_y[0] = tiles_x[...]
    for d in range(1, CHIPS_Y):
        send(tiles_x, tiles_y.at[d], 1, peer(dy=d))
    all_of(tiles_y.at[1:CHIPS_Y], 1).wait_recv()

    n_rows = CHIPS_Y * OWNERS * BLOCK
    high, low = split(tiles_y[...].reshape(n_rows, LANES))
    lane_r = lax.broadcasted_iota(jnp.int32, (n_rows, LANES), 1) % GROUP
    row_r = lax.broadcasted_iota(jnp.int32, (n_rows, LANES), 0) % BLOCK
    group_r = (lane_r // BLOCK).astype(F32)
    same_row = (lane_r % BLOCK) == row_r
    lane64 = lax.broadcasted_iota(jnp.int32, (GROUP, LANES), 1)
    total_spectrum = []
    for j in range(pairs):
        part = slice(j * LANES, (j + 1) * LANES)
        values = mm(high, spread[:, part]) + mm(low, spread[:, part])
        p_of = mm(high, spread[:, width + j * LANES : width + (j + 1) * LANES])
        q_of = mm(high, spread[:, 2 * width + j * LANES : 2 * width + (j + 1) * LANES])
        values = jnp.where(q_of == group_r, values, 0.0)
        place = jnp.where(same_row & (p_of == group_r), 1.0, 0.0).astype(BF16)
        v_high, v_low = split(values)
        dims = (((0,), (0,)), ((), ()))
        both = lax.dot_general(place, v_high, dims, preferred_element_type=F32) + lax.dot_general(
            place, v_low, dims, preferred_element_type=F32
        )
        total_spectrum.append(jnp.where(lane64 >= GROUP, both[GROUP:, :], both[:GROUP, :]))

    squares = jnp.zeros((BLOCK, LANES), F32)
    for part in total_spectrum:
        for p in range(SIDE):
            piece = part[p * BLOCK : (p + 1) * BLOCK, :]
            squares = squares + piece * piece
    sums_x[0] = squares
    for i, (dx, dc) in enumerate(group_x, start=1):
        send(sums_x.at[0], sums_x.at[i], 2, peer(dx=dx, dc=dc))

    high, low = split(jnp.concatenate(total_spectrum, axis=0))
    wide = mm(jnp.concatenate([high, low, high], axis=1), right_inv)
    high, low = split(jnp.concatenate([wide[j * GROUP : (j + 1) * GROUP, :] for j in range(pairs)], axis=1))
    total_ref[mine] = mm(left_inv, jnp.concatenate([high, low, high], axis=0))

    def gather(slot, i, other):
        return pltpu.make_async_remote_copy(
            src_ref=total_ref.at[slot], dst_ref=total_ref.at[slot],
            send_sem=gather_send.at[i], recv_sem=gather_recv.at[i], device_id=other, device_id_type=MESH,
        )

    sends = [gather(mine, d, peer(dx=d)) for d in (1, 3, 2)] + [gather(mine, 4, peer(dc=1))]
    for copy in sends:
        copy.start()

    all_of(sums_x.at[1:OWNERS], 2).wait_recv()
    sums_ref[0] = jnp.sum(sums_x[...], axis=0)
    for d in range(1, SECTIONS):
        send(sums_ref.at[0], sums_ref.at[d], 3, peer(dz=d))

    for d in (1, 3, 2):
        slot = ((x + CHIPS_X - d) % CHIPS_X) * CORES + core
        gather(slot, d, peer(dx=d)).wait_recv()
        copy = gather(slot, 4 + d, peer(dc=1))
        copy.start()
        sends.append(copy)
    for d in (0, 1, 3, 2):
        slot = ((x + CHIPS_X - d) % CHIPS_X) * CORES + (core + 1) % CORES
        gather(slot, 4 + d, peer(dc=1)).wait_recv()

    all_of(sums_ref.at[1:SECTIONS], 3).wait_recv()
    all_of(compact.at[1:OWNERS], 0).wait_send()
    all_of(tiles_y.at[1:CHIPS_Y], 1).wait_send()
    all_of(sums_x.at[1:OWNERS], 2).wait_send()
    all_of(sums_ref.at[1:SECTIONS], 3).wait_send()
    for copy in sends:
        copy.wait_send()


def per_device(gradients, momentum, keep_block):
    local_rows, columns = gradients.shape[1:]
    pairs = columns // (OWNERS * LANES)
    width = pairs * LANES
    tables = jnp.asarray(constant_tables())
    entry_count = float(local_rows * lax.axis_size("section") * columns)
    dma = pltpu.SemaphoreType.DMA
    new_momentum, total, sums = pl.pallas_call(
        functools.partial(kernel, pairs),
        out_shape=(
            pltpu.VMEM((local_rows, columns), F32),
            pltpu.VMEM((OWNERS, local_rows, width), F32),
            pltpu.VMEM((SECTIONS, BLOCK, LANES), F32),
        ),
        in_specs=[pl.BlockSpec(memory_space=pltpu.HBM)] * 4,
        out_specs=(pl.BlockSpec(memory_space=pltpu.VMEM),) * 3,
        scratch_shapes=[
            pltpu.SMEM(keep_block.shape[1:], jnp.int32),
            pltpu.VMEM((local_rows, columns), BF16),
            pltpu.VMEM((local_rows, columns), F32),
            pltpu.VMEM(tables.shape, BF16),
            pltpu.VMEM((OWNERS * BLOCK, width), F32),
            pltpu.VMEM((width, LANES), BF16),
            pltpu.VMEM((LANES, 3 * width), BF16),
            pltpu.VMEM((OWNERS, BLOCK, LANES), F32),
            pltpu.VMEM((OWNERS, BLOCK, LANES), F32),
            pltpu.VMEM((CHIPS_Y, OWNERS, BLOCK, LANES), F32),
            pltpu.VMEM((OWNERS, BLOCK, LANES), F32),
            dma((5,)), dma, dma((4,)), dma((4,)), dma((OWNERS,)), dma((OWNERS,)),
        ],
        compiler_params=pltpu.CompilerParams(collective_id=0, has_side_effects=True, vmem_limit_bytes=56 << 20),
        name="kept_blocks_step",
    )(keep_block[0], gradients[0], momentum[0], tables)
    scale = lax.rsqrt(jnp.sum(sums) / entry_count + epsilon)
    update = (jnp.transpose(total, (1, 0, 2)).reshape(local_rows, columns) * scale).astype(BF16)
    return new_momentum[None], update


def solution(mesh):
    placed = (
        P("replica", "section", None),
        P("replica", "section", None),
        P("replica", "section", None),
    )
    return jax.shard_map(
        per_device,
        mesh=mesh,
        in_specs=placed,
        out_specs=(P("replica", "section", None), P("section", None)),
        check_vma=False,
    )
```

time: 53.2 us -> 43.3 us (0.81)
  Pallas kernels: 49 us -> 39.2 us
  local copies, waits for them, and re-layouts: 3.37 us -> 1.96 us
  other arithmetic: 0 us -> 0.7 us
  between operations: 0.65 us -> 1.34 us
    pallas_call x1, Pallas kernels: 49 us -> 39.2 us  [per_device(): pl.pallas_call(functools.partial(kernel, pairs), out_shape=(pltpu.VMEM((l...]
    unnamed x4 -> x1, local copies, waits for them, and re-layouts: 3.37 us -> 1.06 us
    convert_element_type x0 -> x1, local copies, waits for them, and re-layouts: none -> 0.9 us  [per_device(): (jnp.transpose(total, (1, 0, 2)).reshape(local_rows, columns) * scale).as...]
    reduce_sum x0 -> x1, other arithmetic: none -> 0.61 us  [per_device(): scale = lax.rsqrt(jnp.sum(sums) / entry_count + epsilon)]
where the time goes in v2:
time: 43.3 us; the launch traced here: 43.2 us
  Pallas kernels  39.2 us (91%)
  local copies, waits for them, and re-layouts  1.96 us (5%)
  between operations  1.34 us (3%)
  other arithmetic  0.7 us (2%)
    pallas_call x1, Pallas kernels, per_device(): pl.pallas_call(functools.partial(kernel, pairs), out_shape=(pltpu.VMEM((l...  39.2 us
    unnamed x1, local copies, waits for them, and re-layouts  1.06 us
    convert_element_type x1, local copies, waits for them, and re-layouts, per_device(): (jnp.transpose(total, (1, 0, 2)).reshape(local_rows, columns) * scale).as...  0.9 us

profile of v2, /device:TPU:1, one launch (start us, length us, event | category | flops | bytes accessed | tf_op | source)
XLA Modules:
  0.0 43.2 jit_solution(17939630581756075910)
XLA Ops:
  0.6 39.2 %kept_blocks_step.1 = (f32[64,5120]{1,0:T(8,128)S(1)}, f32[8,64,640]{2,1,0:T(8,128)S(1)}, f32[8,8,128]{2,1,0:T(8,128)S(1)}) custom-call(s32[1,80]{1,0:T(1,128)} %bitcast.12, bf16[64,5120]{1,0:T(8,128)(2,1)} %bitcast.10, f32[64,5120]{1,0:T(8,128)} %bitcast.9, bf16[1024,128]{1,0:T(8,128)(2,1)} %constant.9.clone.tab_ref), custom_call_target="tpu_custom_call" | custom-call | tf_op jit(solution)/shard_map/kept_blocks_step/pallas_call | solution.py:299
  39.8 0.6 %reduce_sum.9 = f32[]{:T(128)} reduce(f32[8,8,128]{2,1,0:T(8,128)S(1)} %get-tuple-element.7, f32[]{:T(128)} %constant.2.clone.1), dimensions={0,1,2}, to_apply=%region_0.0 | reduce | flops 8191 | bytes 32776 | tf_op jit(solution)/shard_map/reduce_sum | solution.py:325
  41.1 0.1 fusion
  41.2 0.9 %copy.7 = bf16[8,8,8,640]{3,2,0,1:T(8,128)(2,1)} copy(bf16[8,8,8,640]{3,2,1,0:T(8,128)(2,1)S(1)} %fusion) | data formatting | bytes 1310720 | tf_op jit(solution)/shard_map/convert_element_type | solution.py:326
  42.1 1.1 %copy.9 = f32[1,64,5120]{2,1,0:T(8,128)} copy(f32[1,64,5120]{2,1,0:T(8,128)S(1)} %bitcast.8) | data formatting | bytes 2621440

commit v3 on v2

--- a/solution.py
+++ b/solution.py
@@ -48,7 +48,10 @@
         wide = np.concatenate([high, high, low, np.zeros_like(low)], axis=1)
         return np.concatenate([wide[:, :LANES], wide[:, LANES:]], axis=0)
 
-    return np.concatenate([right(basis.T), right(basis), left(basis), left(basis.T)], axis=0)
+    by_row_in_block = np.arange(GROUP).reshape(SIDE, BLOCK).T.reshape(-1)
+    return np.concatenate(
+        [right(basis.T), right(basis), left(basis), left(basis.T), left(basis.T[:, by_row_in_block])], axis=0
+    )
 
 
 def split(values):
@@ -78,7 +81,9 @@
         px, py, pc = (x + dx) % CHIPS_X, (y + dy) % CHIPS_Y, (core + dc) % CORES
         return ((px * CHIPS_Y + py) * CORES + pc, (section + dz) % SECTIONS)
 
-    group_x = [(dx, dc) for dx in range(CHIPS_X) for dc in range(CORES)][1:]
+    group_x = sorted([(dx, dc) for dx in range(CHIPS_X) for dc in range(CORES)][1:], key=lambda o: (-min(o[0], CHIPS_X - o[0]), -o[1]))
+    group_y = sorted(range(1, CHIPS_Y), key=lambda d: -min(d, CHIPS_Y - d))
+    group_z = sorted(range(1, SECTIONS), key=lambda d: -min(d, SECTIONS - d))
 
     half = OWNERS // 2 * width
     loads = []
@@ -107,17 +112,16 @@
         pl.semaphore_signal(barrier, inc=1, device_id=other, device_id_type=MESH)
 
     lane8 = lax.broadcasted_iota(jnp.int32, (BLOCK, LANES), 1)
+    row8 = lax.broadcasted_iota(jnp.int32, (BLOCK, LANES), 0)
     upper = lane8 >= GROUP
     lane_q = (lane8 % GROUP) // BLOCK
-    row_f = lax.broadcasted_iota(jnp.int32, (width, LANES), 0)
-    lane_f = lax.broadcasted_iota(jnp.int32, (width, LANES), 1)
-    fold[...] = jnp.where((row_f // GROUP) * BLOCK + row_f % BLOCK == lane_f, 1.0, 0.0).astype(BF16)
-    row_t = lax.broadcasted_iota(jnp.int32, (LANES, width), 0)
-    lane_t = lax.broadcasted_iota(jnp.int32, (LANES, width), 1)
-    block_t = lane_t // GROUP
-    spread[:, 0:width] = jnp.where(row_t == block_t * BLOCK + lane_t % BLOCK, 1.0, 0.0).astype(BF16)
-    spread[:, width : 2 * width] = jnp.where(row_t == BLOCK * n_blocks + block_t, 1.0, 0.0).astype(BF16)
-    spread[:, 2 * width : 3 * width] = jnp.where(row_t == (BLOCK + 1) * n_blocks + block_t, 1.0, 0.0).astype(BF16)
+    row_g = lax.broadcasted_iota(jnp.int32, (LANES, LANES), 0)
+    lane_g = lax.broadcasted_iota(jnp.int32, (LANES, LANES), 1)
+    same_hm = (row_g // GROUP == lane_g // GROUP) & (row_g % BLOCK == lane_g % BLOCK)
+    fold[...] = jnp.where(same_hm, 1.0, 0.0).astype(BF16)
+    for i in range(BLOCK):
+        of_row = same_hm & ((row_g % GROUP) // BLOCK == i)
+        spread[:, i * LANES : (i + 1) * LANES] = jnp.where(of_row, 1.0, 0.0).astype(BF16)
 
     kb_load.wait()
     tab_load.wait()
@@ -125,6 +129,7 @@
     right_inv = tab[384:768, :]
     left_fwd = jnp.concatenate([tab[768:832, :], tab[832:896, 0:64]], axis=1)
     left_inv = jnp.concatenate([tab[896:960, :], tab[960:1024, 0:64]], axis=1)
+    left_inv_ip = jnp.concatenate([tab[1024:1088, :], tab[1088:1152, 0:64]], axis=1)
 
     def block_pair(s, j):
         c = s * n_blocks + 2 * j
@@ -160,17 +165,21 @@
     for s in range(OWNERS):
         for j in range(pairs):
             row = (s * pairs + j) * BLOCK
-            kept = jnp.where(q_lanes(s, j) == lane_q, spectrum[row : row + BLOCK, :], 0.0)
-            masked[s * BLOCK : (s + 1) * BLOCK, j * LANES : (j + 1) * LANES] = kept
-
-    high, low = split(masked[...])
-    packed = mm(high, fold[...]) + mm(low, fold[...])
+            masked[row : row + BLOCK, :] = jnp.where(q_lanes(s, j) == lane_q, spectrum[row : row + BLOCK, :], 0.0)
+
+    kept_high, kept_low = split(masked[...])
+    folded = mm(kept_high, fold[...]) + mm(kept_low, fold[...])
     for s in range(OWNERS):
-        tile = packed[s * BLOCK : (s + 1) * BLOCK, :]
+        tile = jnp.zeros((BLOCK, LANES), F32)
+        for j in range(pairs):
+            row = (s * pairs + j) * BLOCK
+            piece = jnp.where(row8 == lane_q, folded[row : row + BLOCK, :], 0.0)
+            for shift in (4, 2, 1):
+                piece = piece + pltpu.roll(piece, shift, 0)
+            tile = jnp.where(row8 == j, piece, tile)
         for b in range(n_blocks):
-            k = kb_ref[0, s * n_blocks + b]
-            tile = jnp.where(lane8 == BLOCK * n_blocks + b, (k // SIDE).astype(F32), tile)
-            tile = jnp.where(lane8 == (BLOCK + 1) * n_blocks + b, (k % SIDE).astype(F32), tile)
+            number = kb_ref[0, s * n_blocks + b].astype(F32)
+            tile = jnp.where((row8 == pairs) & (lane8 == b), number, tile)
         compact[s] = tile
 
     pl.semaphore_wait(barrier, len(everyone))
@@ -190,17 +199,10 @@
 
     for i, (dx, dc) in enumerate(group_x, start=1):
         px, pc = (x + dx) % CHIPS_X, (core + dc) % CORES
-        send(compact.at[px * CORES + pc], tiles_x.at[i], 0, peer(dx=dx, dc=dc))
-    tiles_x[0] = compact[mine]
-
-    wide = []
-    for s in range(OWNERS):
-        stacked = jnp.concatenate(
-            [masked[s * BLOCK : (s + 1) * BLOCK, j * LANES : (j + 1) * LANES] for j in range(pairs)], axis=0
-        )
-        wide.append(stacked)
-    high, low = split(jnp.concatenate(wide, axis=0))
-    wide = mm(jnp.concatenate([high, low, high], axis=1), right_inv)
+        send(compact.at[px * CORES + pc], tiles_x.at[pl.ds(i * BLOCK, BLOCK)], 0, peer(dx=dx, dc=dc))
+    tiles_x[0:BLOCK, :] = compact[mine]
+
+    wide = mm(jnp.concatenate([kept_high, kept_low, kept_high], axis=1), right_inv)
     for s in range(OWNERS):
         cols = slice(s * width, (s + 1) * width)
         placed = []
@@ -212,48 +214,57 @@
         high, low = split(jnp.concatenate(placed, axis=1))
         nm_ref[:, cols] = nm_ref[:, cols] - mm(left_inv, jnp.concatenate([high, low, high], axis=0))
 
-    all_of(tiles_x.at[1:OWNERS], 0).wait_recv()
-
-    tiles_y[0] = tiles_x[...]
-    for d in range(1, CHIPS_Y):
-        send(tiles_x, tiles_y.at[d], 1, peer(dy=d))
-    all_of(tiles_y.at[1:CHIPS_Y], 1).wait_recv()
-
-    n_rows = CHIPS_Y * OWNERS * BLOCK
-    high, low = split(tiles_y[...].reshape(n_rows, LANES))
-    lane_r = lax.broadcasted_iota(jnp.int32, (n_rows, LANES), 1) % GROUP
-    row_r = lax.broadcasted_iota(jnp.int32, (n_rows, LANES), 0) % BLOCK
-    group_r = (lane_r // BLOCK).astype(F32)
-    same_row = (lane_r % BLOCK) == row_r
+    all_of(tiles_x.at[BLOCK:], 0).wait_recv()
+
+    n_x = OWNERS * BLOCK
+    for d in group_y:
+        send(tiles_x, tiles_y.at[pl.ds(d * n_x, n_x)], 1, peer(dy=d))
+    tiles_y[0:n_x, :] = tiles_x[...]
+    all_of(tiles_y.at[n_x:], 1).wait_recv()
+
+    n_replica = CHIPS_Y * OWNERS
+    numbers = tiles_y[pl.ds(pairs, n_replica, stride=BLOCK), :].astype(BF16)
+    row_n = lax.broadcasted_iota(jnp.int32, (2 * BLOCK, LANES), 0)
+    lane_n = lax.broadcasted_iota(jnp.int32, (2 * BLOCK, LANES), 1)
+    pick = jnp.where(row_n == lane_n, 1.0, 0.0).astype(BF16)
+    numbers = lax.dot_general(pick, numbers, (((1,), (1,)), ((), ())), preferred_element_type=F32)
+    place = lax.broadcasted_iota(jnp.int32, (GROUP, n_replica), 0).astype(F32)
     lane64 = lax.broadcasted_iota(jnp.int32, (GROUP, LANES), 1)
-    total_spectrum = []
+    row64 = lax.broadcasted_iota(jnp.int32, (GROUP, LANES), 0)
+    squares = jnp.zeros((BLOCK, LANES), F32)
+    spectra = []
     for j in range(pairs):
-        part = slice(j * LANES, (j + 1) * LANES)
-        values = mm(high, spread[:, part]) + mm(low, spread[:, part])
-        p_of = mm(high, spread[:, width + j * LANES : width + (j + 1) * LANES])
-        q_of = mm(high, spread[:, 2 * width + j * LANES : 2 * width + (j + 1) * LANES])
-        values = jnp.where(q_of == group_r, values, 0.0)
-        place = jnp.where(same_row & (p_of == group_r), 1.0, 0.0).astype(BF16)
-        v_high, v_low = split(values)
-        dims = (((0,), (0,)), ((), ()))
-        both = lax.dot_general(place, v_high, dims, preferred_element_type=F32) + lax.dot_general(
-            place, v_low, dims, preferred_element_type=F32
-        )
-        total_spectrum.append(jnp.where(lane64 >= GROUP, both[GROUP:, :], both[:GROUP, :]))
-
-    squares = jnp.zeros((BLOCK, LANES), F32)
-    for part in total_spectrum:
+        high, low = split(tiles_y[pl.ds(j, n_replica, stride=BLOCK), :])
+        where_to = jnp.concatenate(
+            [jnp.where(numbers[b : b + 1, :] == place, 1.0, 0.0).astype(BF16) for b in (2 * j, 2 * j + 1)], axis=0
+        )
+        both = mm(jnp.concatenate([where_to, where_to], axis=1), jnp.concatenate([high, low], axis=0))
+        both = jnp.where(lane64 >= GROUP, both[GROUP:, :], both[:GROUP, :])
+        spectra.append(both)
         for p in range(SIDE):
-            piece = part[p * BLOCK : (p + 1) * BLOCK, :]
+            piece = both[p * BLOCK : (p + 1) * BLOCK, :]
             squares = squares + piece * piece
     sums_x[0] = squares
     for i, (dx, dc) in enumerate(group_x, start=1):
         send(sums_x.at[0], sums_x.at[i], 2, peer(dx=dx, dc=dc))
 
-    high, low = split(jnp.concatenate(total_spectrum, axis=0))
+    row_p = lax.broadcasted_iota(jnp.int32, (BLOCK, LANES), 0)
+    gather_p = jnp.where((lane8 % GROUP) // SIDE == row_p, 1.0, 0.0).astype(BF16)
+    same_q = row64 % SIDE == (lane64 % GROUP) // BLOCK
+    stacked = []
+    for j in range(pairs):
+        high, low = split(spectra[j])
+        both = mm(high, spread[...]) + mm(low, spread[...])
+        both = jnp.concatenate(
+            [jnp.where(same_q, both[:, i * LANES : (i + 1) * LANES], 0.0) for i in range(BLOCK)], axis=1
+        )
+        high, low = split(both)
+        both = mm(gather_p, jnp.concatenate([high, low], axis=0))
+        stacked += [both[:, i * LANES : (i + 1) * LANES] for i in range(BLOCK)]
+    high, low = split(jnp.concatenate(stacked, axis=0))
     wide = mm(jnp.concatenate([high, low, high], axis=1), right_inv)
     high, low = split(jnp.concatenate([wide[j * GROUP : (j + 1) * GROUP, :] for j in range(pairs)], axis=1))
-    total_ref[mine] = mm(left_inv, jnp.concatenate([high, low, high], axis=0))
+    total_ref[mine] = mm(left_inv_ip, jnp.concatenate([high, low, high], axis=0))
 
     def gather(slot, i, other):
         return pltpu.make_async_remote_copy(
@@ -267,7 +278,7 @@
 
     all_of(sums_x.at[1:OWNERS], 2).wait_recv()
     sums_ref[0] = jnp.sum(sums_x[...], axis=0)
-    for d in range(1, SECTIONS):
+    for d in group_z:
         send(sums_ref.at[0], sums_ref.at[d], 3, peer(dz=d))
 
     for d in (1, 3, 2):
@@ -282,11 +293,27 @@
 
     all_of(sums_ref.at[1:SECTIONS], 3).wait_recv()
     all_of(compact.at[1:OWNERS], 0).wait_send()
-    all_of(tiles_y.at[1:CHIPS_Y], 1).wait_send()
+    all_of(tiles_y.at[n_x:], 1).wait_send()
     all_of(sums_x.at[1:OWNERS], 2).wait_send()
     all_of(sums_ref.at[1:SECTIONS], 3).wait_send()
     for copy in sends:
         copy.wait_send()
+
+
+def finish(entry_count, width, nm_ref, total_ref, sums_ref, nm_out, upd_out, upd, sem):
+    stores = [pltpu.make_async_copy(nm_ref, nm_out, sem.at[0])]
+    stores[0].start()
+    squares = jnp.sum(sums_ref[...], axis=0)
+    squares = jnp.sum(jnp.sum(squares, axis=0, keepdims=True), axis=1, keepdims=True)
+    scale = lax.rsqrt(squares / entry_count + epsilon)
+    for k in range(OWNERS // 2):
+        for s in (2 * k, 2 * k + 1):
+            upd[:, s * width : (s + 1) * width] = (total_ref[s] * scale).astype(BF16)
+        cols = slice(2 * k * width, 2 * (k + 1) * width)
+        stores.append(pltpu.make_async_copy(upd.at[:, cols], upd_out.at[:, cols], sem.at[1 + k]))
+        stores[-1].start()
+    for copy in stores:
+        copy.wait()
 
 
 def per_device(gradients, momentum, keep_block):
@@ -310,20 +337,31 @@
             pltpu.VMEM((local_rows, columns), BF16),
             pltpu.VMEM((local_rows, columns), F32),
             pltpu.VMEM(tables.shape, BF16),
-            pltpu.VMEM((OWNERS * BLOCK, width), F32),
-            pltpu.VMEM((width, LANES), BF16),
-            pltpu.VMEM((LANES, 3 * width), BF16),
+            pltpu.VMEM((OWNERS * pairs * BLOCK, LANES), F32),
+            pltpu.VMEM((LANES, LANES), BF16),
+            pltpu.VMEM((LANES, BLOCK * LANES), BF16),
             pltpu.VMEM((OWNERS, BLOCK, LANES), F32),
-            pltpu.VMEM((OWNERS, BLOCK, LANES), F32),
-            pltpu.VMEM((CHIPS_Y, OWNERS, BLOCK, LANES), F32),
+            pltpu.VMEM((OWNERS * BLOCK, LANES), F32),
+            pltpu.VMEM((CHIPS_Y * OWNERS * BLOCK, LANES), F32),
             pltpu.VMEM((OWNERS, BLOCK, LANES), F32),
             dma((5,)), dma, dma((4,)), dma((4,)), dma((OWNERS,)), dma((OWNERS,)),
         ],
         compiler_params=pltpu.CompilerParams(collective_id=0, has_side_effects=True, vmem_limit_bytes=56 << 20),
         name="kept_blocks_step",
     )(keep_block[0], gradients[0], momentum[0], tables)
-    scale = lax.rsqrt(jnp.sum(sums) / entry_count + epsilon)
-    update = (jnp.transpose(total, (1, 0, 2)).reshape(local_rows, columns) * scale).astype(BF16)
+    hbm = pl.BlockSpec(memory_space=pltpu.HBM)
+    new_momentum, update = pl.pallas_call(
+        functools.partial(finish, entry_count, width),
+        out_shape=(
+            jax.ShapeDtypeStruct((local_rows, columns), F32),
+            jax.ShapeDtypeStruct((local_rows, columns), BF16),
+        ),
+        in_specs=[pl.BlockSpec(memory_space=pltpu.VMEM)] * 3,
+        out_specs=(hbm, hbm),
+        scratch_shapes=[pltpu.VMEM((local_rows, columns), BF16), dma((1 + OWNERS // 2,))],
+        compiler_params=pltpu.CompilerParams(vmem_limit_bytes=32 << 20),
+        name="scale_and_store",
+    )(new_momentum, total, sums)
     return new_momentum[None], update
 
 

time: 43.3 us -> 38.6 us (0.89)
  local copies, waits for them, and re-layouts: 1.96 us -> 0 us
  Pallas kernels: 39.2 us -> 37.5 us
  between operations: 1.34 us -> 0.64 us
  other arithmetic: 0.7 us -> 0 us
    pallas_call x1, Pallas kernels: 39.2 us -> 36.2 us  [per_device(): pl.pallas_call(functools.partial(kernel, pairs), out_shape=(pltpu.VMEM((l...]
    pallas_call x0 -> x1, Pallas kernels: none -> 1.31 us  [per_device(): pl.pallas_call(functools.partial(finish, entry_count, width), out_shape=(...]
    unnamed x1 -> x0, local copies, waits for them, and re-layouts: 1.06 us -> none
    convert_element_type x1 -> x0, local copies, waits for them, and re-layouts: 0.9 us -> none  [per_device(): (jnp.transpose(total, (1, 0, 2)).reshape(local_rows, columns) * scale).as...]
    reduce_sum x1 -> x0, other arithmetic: 0.61 us -> none  [per_device(): scale = lax.rsqrt(jnp.sum(sums) / entry_count + epsilon)]
where the time goes in v3:
time: 38.6 us; the launch traced here: 38.2 us
  Pallas kernels  37.5 us (97%)
  between operations  0.64 us (2%)
    pallas_call x1, Pallas kernels, per_device(): pl.pallas_call(functools.partial(kernel, pairs), out_shape=(pltpu.VMEM((l...  36.2 us
    pallas_call x1, Pallas kernels, per_device(): pl.pallas_call(functools.partial(finish, entry_count, width), out_shape=(...  1.31 us

profile of v3, /device:TPU:1, one launch (start us, length us, event | category | flops | bytes accessed | tf_op | source)
XLA Modules:
  0.0 38.2 jit_solution(14080496290949318645)
XLA Ops:
  0.6 36.2 %kept_blocks_step.1 = (f32[64,5120]{1,0:T(8,128)S(1)}, f32[8,64,640]{2,1,0:T(8,128)S(1)}, f32[8,8,128]{2,1,0:T(8,128)S(1)}) custom-call(s32[1,80]{1,0:T(1,128)} %bitcast.6, bf16[64,5120]{1,0:T(8,128)(2,1)} %bitcast.5, f32[64,5120]{1,0:T(8,128)} %bitcast.4, bf16[1152,128]{1,0:T(8,128)(2,1)} %constant.2.clone.tab_ref), custom_call_target="tpu_custom_call" | custom-call | tf_op jit(solution)/shard_map/kept_blocks_step/pallas_call | solution.py:326
  36.9 1.3 %scale_and_store.1 = (f32[64,5120]{1,0:T(8,128)}, bf16[64,5120]{1,0:T(8,128)(2,1)}) custom-call(f32[64,5120]{1,0:T(8,128)S(1)} %get-tuple-element.7.nm_ref, f32[8,64,640]{2,1,0:T(8,128)S(1)} %get-tuple-element.8.total_ref, f32[8,8,128]{2,1,0:T(8,128)S(1)} %get-tuple-element.9.sums_ref), custom_call_target="tpu_custom_call" | custom-call | tf_op jit(solution)/shard_map/scale_and_store/pallas_call | solution.py:353

commit v4 on v3

v4 whole, which is shorter than its diff:
```python
import functools

import jax
import jax.numpy as jnp
import ml_dtypes
import numpy as np
from jax import lax
from jax.experimental import pallas as pl
from jax.experimental.pallas import tpu as pltpu
from jax.sharding import PartitionSpec as P

GROUP = 64
BLOCK = 8
SIDE = GROUP // BLOCK
LANES = 128
CHIPS_X, CHIPS_Y, CORES, SECTIONS = 4, 8, 2, 8
OWNERS = CHIPS_X * CORES
MESH = pl.DeviceIdType.MESH
ROWS_SENT = 48
TOP = 32000.0
F32, BF16 = jnp.float32, jnp.bfloat16

momentum_decay = 0.9
epsilon = 1e-06


def dct_basis():
    k = np.arange(GROUP, dtype=np.float64)[:, None]
    n = np.arange(GROUP, dtype=np.float64)[None, :]
    basis = np.sqrt(2.0 / GROUP) * np.cos(np.pi * (2.0 * n + 1.0) * k / (2.0 * GROUP))
    basis[0] /= np.sqrt(2.0)
    return basis.astype(np.float32)


def two_terms(values):
    high = values.astype(ml_dtypes.bfloat16)
    low = (values - high.astype(np.float32)).astype(ml_dtypes.bfloat16)
    return high, low


def constant_tables():
    basis = dct_basis()

    def right(matrix):
        high, low = two_terms(np.kron(np.eye(2, dtype=np.float32), matrix))
        return np.concatenate([high, high, low], axis=0)

    def left(matrix):
        high, low = two_terms(matrix)
        wide = np.concatenate([high, high, low, np.zeros_like(low)], axis=1)
        return np.concatenate([wide[:, :LANES], wide[:, LANES:]], axis=0)

    by_row_in_block = np.arange(GROUP).reshape(SIDE, BLOCK).T.reshape(-1)
    return np.concatenate(
        [right(basis.T), right(basis), left(basis), left(basis.T), left(basis.T[:, by_row_in_block])], axis=0
    )


def column_table():
    basis = dct_basis().reshape(SIDE, BLOCK, GROUP)
    table = np.einsum("qmn,ij->qimjn", basis, np.eye(BLOCK, dtype=np.float32))
    terms = np.stack(two_terms(table.reshape(SIDE * GROUP, BLOCK * GROUP)))
    return terms.reshape(2, SIDE * GROUP, BLOCK * GROUP // LANES, LANES).transpose(0, 2, 1, 3).reshape(-1, LANES)


def split(values):
    high = values.astype(BF16)
    low = (values - high.astype(F32)).astype(BF16)
    return high, low


def mm(a, b):
    return jnp.dot(a, b, preferred_element_type=F32)


def kernel(
    pairs, kb_hbm, g_ref, m_ref, tab_ref, col_ref, nm_ref, total_ref, sums_ref,
    kb_ref, kb_row, g_buf, m_buf, tab, col_tab, masked, fold, tiles, wide_tiles, spec_high, spec_low, total_high, total_low,
    load_sem, kb_sem, send_sem, y_recv, x_recv, core_recv, z_recv,
):
    width = pairs * LANES
    n_blocks = 2 * pairs
    replica, section = lax.axis_index("replica"), lax.axis_index("section")
    x = replica // (CHIPS_Y * CORES)
    y = (replica // CORES) % CHIPS_Y
    core = replica % CORES

    def peer(dx=0, dy=0, dc=0, dz=0):
        px, py, pc = (x + dx) % CHIPS_X, (y + dy) % CHIPS_Y, (core + dc) % CORES
        return ((px * CHIPS_Y + py) * CORES + pc, (section + dz) % SECTIONS)

    n_pairs = OWNERS * pairs
    group_y = sorted(range(1, CHIPS_Y), key=lambda d: -min(d, CHIPS_Y - d))
    group_x = (2, 1, 3)
    row_order = (0, 2, 3, 1, 6, 7, 5, 4)

    half = OWNERS // 2 * width
    loads = []
    kb_load = pltpu.make_async_copy(kb_hbm, kb_ref, kb_sem.at[0])
    kb_row_load = pltpu.make_async_copy(kb_hbm, kb_row, kb_sem.at[1])
    tab_load = pltpu.make_async_copy(tab_ref, tab, load_sem.at[4])
    for h in range(2):
        cols = slice(h * half, (h + 1) * half)
        pair = (
            pltpu.make_async_copy(m_ref.at[:, cols], m_buf.at[:, cols], load_sem.at[2 * h]),
            pltpu.make_async_copy(g_ref.at[:, cols], g_buf.at[:, cols], load_sem.at[2 * h + 1]),
        )
        loads.append(pair)
        pair[0].start()
        pair[1].start()
        if h == 0:
            kb_load.start()
            kb_row_load.start()
            tab_load.start()

    col_load = pltpu.make_async_copy(col_ref, col_tab, load_sem.at[5])
    col_load.start()

    barrier = pltpu.get_barrier_semaphore()
    everyone = (
        [peer(dx=d) for d in group_x]
        + [peer(dy=d) for d in group_y]
        + [peer(dz=d) for d in range(1, SECTIONS)]
        + [peer(dc=1)]
    )
    for other in everyone:
        pl.semaphore_signal(barrier, inc=1, device_id=other, device_id_type=MESH)

    lane8 = lax.broadcasted_iota(jnp.int32, (BLOCK, LANES), 1)
    row8 = lax.broadcasted_iota(jnp.int32, (BLOCK, LANES), 0)
    upper = lane8 >= GROUP
    lane_q = (lane8 % GROUP) // BLOCK
    row_g = lax.broadcasted_iota(jnp.int32, (LANES, LANES), 0)
    lane_g = lax.broadcasted_iota(jnp.int32, (LANES, LANES), 1)
    same_hm = (row_g // GROUP == lane_g // GROUP) & (row_g % BLOCK == lane_g % BLOCK)
    fold[...] = jnp.where(same_hm, 1.0, 0.0).astype(BF16)

    kb_load.wait()
    kb_row_load.wait()
    numbers = jnp.concatenate([kb_row[...].astype(F32), jnp.zeros((1, LANES - kb_row.shape[1]), F32)], axis=1)
    tab_load.wait()
    right_fwd = tab[0:384, :]
    right_inv = tab[384:768, :]
    left_fwd = jnp.concatenate([tab[768:832, :], tab[832:896, 0:64]], axis=1)
    left_inv = jnp.concatenate([tab[896:960, :], tab[960:1024, 0:64]], axis=1)
    left_inv_ip = jnp.concatenate([tab[1024:1088, :], tab[1088:1152, 0:64]], axis=1)

    def block_pair(s, j):
        c = s * n_blocks + 2 * j
        return kb_ref[0, c], kb_ref[0, c + 1]

    def p_lanes(s, j):
        k0, k1 = block_pair(s, j)
        return jnp.where(upper, k1 // SIDE, k0 // SIDE)

    def q_lanes(s, j):
        k0, k1 = block_pair(s, j)
        return jnp.where(upper, k1 % SIDE, k0 % SIDE)

    chosen = []
    for s in range(OWNERS):
        if s % (OWNERS // 2) == 0:
            for copy in loads[s // (OWNERS // 2)]:
                copy.wait()
        cols = slice(s * width, (s + 1) * width)
        moments = momentum_decay * m_buf[:, cols] + g_buf[:, cols].astype(F32)
        nm_ref[:, cols] = moments
        high, low = split(moments)
        rows = mm(left_fwd, jnp.concatenate([high, low, high], axis=0))
        for j in range(pairs):
            p_of = p_lanes(s, j)
            picked = jnp.zeros((BLOCK, LANES), F32)
            for p in range(SIDE):
                picked = jnp.where(p_of == p, rows[p * BLOCK : (p + 1) * BLOCK, j * LANES : (j + 1) * LANES], picked)
            chosen.append(picked)

    high, low = split(jnp.concatenate(chosen, axis=0))
    spectrum = mm(jnp.concatenate([high, low, high], axis=1), right_fwd)
    for s in range(OWNERS):
        for j in range(pairs):
            row = (s * pairs + j) * BLOCK
            masked[row : row + BLOCK, :] = jnp.where(q_lanes(s, j) == lane_q, spectrum[row : row + BLOCK, :], 0.0)

    kept_high, kept_low = split(masked[...])
    folded = mm(kept_high, fold[...]) + mm(kept_low, fold[...])
    lines = []
    for k in range(n_pairs):
        piece = jnp.where(row8 == lane_q, folded[k * BLOCK : (k + 1) * BLOCK, :], 0.0)
        for shift in (4, 2, 1):
            piece = piece + pltpu.roll(piece, shift, 0)
        if k % BLOCK == 0:
            lines.append(piece)
        else:
            lines[-1] = jnp.where(row8 == k % BLOCK, piece, lines[-1])

    largest = jnp.abs(lines[0])
    for line in lines[1:]:
        largest = jnp.maximum(largest, jnp.abs(line))
    largest = jnp.max(jnp.max(largest, axis=0, keepdims=True), axis=1, keepdims=True)
    exponent = jnp.ceil(jnp.log2(jnp.maximum(largest, 1e-30)) + 0.01)
    to_code = TOP * jnp.exp2(-exponent)
    coded = [jnp.round(line * to_code) for line in lines]
    coded.append(jnp.where(row8 == 0, numbers, jnp.where(row8 == 1, exponent, 0.0)))
    coded = jnp.concatenate(coded, axis=0).astype(jnp.int32).astype(jnp.int16)
    tiles[y, core, 0] = coded

    pl.semaphore_wait(barrier, len(everyone))

    SEND_Y, SEND_X, SEND_CORE, SEND_Z = range(4)

    def remote(src, dst, which, recv, other):
        return pltpu.make_async_remote_copy(
            src_ref=src, dst_ref=dst, send_sem=send_sem.at[which], recv_sem=recv, device_id=other, device_id_type=MESH
        )

    def received(ref, recv):
        remote(ref, ref, SEND_Y, recv, peer(dc=1)).wait_recv()

    def sent(ref, which):
        remote(ref, ref, which, z_recv, peer(dc=1)).wait_send()

    def along_x(row):
        for d in group_x:
            remote(tiles.at[row, core, 0], tiles.at[row, core, CHIPS_X - d], SEND_X, x_recv.at[row], peer(dx=d)).start()

    def to_core(row):
        received(tiles.at[row, core, 1:CHIPS_X], x_recv.at[row])
        remote(tiles.at[row, core], tiles.at[row, core], SEND_CORE, core_recv.at[row], peer(dc=1)).start()

    for d in group_y:
        remote(tiles.at[y, core, 0], tiles.at[y, core, 0], SEND_Y, y_recv.at[y], peer(dy=d)).start()
    along_x(y)

    wide = mm(jnp.concatenate([kept_high, kept_low, kept_high], axis=1), right_inv)
    for s in range(OWNERS):
        cols = slice(s * width, (s + 1) * width)
        placed = []
        for j in range(pairs):
            p_of = p_lanes(s, j)
            row = (s * pairs + j) * BLOCK
            piece = wide[row : row + BLOCK, :]
            placed.append(jnp.concatenate([jnp.where(p_of == p, piece, 0.0) for p in range(SIDE)], axis=0))
        high, low = split(jnp.concatenate(placed, axis=1))
        nm_ref[:, cols] = nm_ref[:, cols] - mm(left_inv, jnp.concatenate([high, low, high], axis=0))

    lag = 4
    for k in range(CHIPS_Y + lag):
        if k < CHIPS_Y:
            row = row_order[k]

            @pl.when(y != row)
            def _():
                received(tiles.at[row, core, 0], y_recv.at[row])
                along_x(row)

        if k >= lag:
            to_core(row_order[k - lag])
    n_replica = CHIPS_Y * CORES * CHIPS_X
    of_row = CORES * CHIPS_X * ROWS_SENT
    for row in row_order:
        received(tiles.at[row, 1 - core], core_recv.at[row])
        values = tiles[row].reshape(of_row, LANES).astype(jnp.int32).astype(F32)
        wide_tiles[row * of_row : (row + 1) * of_row, :] = values

    def halves(tiles_of):
        firsts, seconds = [], []
        for even, odd in zip(tiles_of[0::2], tiles_of[1::2]):
            firsts.append(jnp.where(upper, pltpu.roll(odd, GROUP, 1), even))
            seconds.append(jnp.where(upper, odd, pltpu.roll(even, GROUP, 1)))
        return jnp.concatenate([jnp.concatenate(firsts, axis=1), jnp.concatenate(seconds, axis=1)], axis=0)

    def of_all(line):
        return wide_tiles[pl.ds(line, n_replica, stride=ROWS_SENT), :]

    row_n = lax.broadcasted_iota(jnp.int32, (2 * n_pairs, LANES), 0)
    lane_n = lax.broadcasted_iota(jnp.int32, (2 * n_pairs, LANES), 1)
    pick = jnp.where(row_n == lane_n, 1.0, 0.0).astype(BF16)
    numbers = lax.dot_general(
        pick, of_all(n_pairs).astype(BF16), (((1,), (1,)), ((), ())), preferred_element_type=F32
    )
    from_code = jnp.exp2(of_all(n_pairs + 1)) * (1.0 / TOP)
    row_place = lax.broadcasted_iota(jnp.int32, (GROUP, n_replica), 0)
    place = ((row_place % BLOCK) * SIDE + row_place // BLOCK).astype(F32)
    lane64 = lax.broadcasted_iota(jnp.int32, (GROUP, LANES), 1)
    squares = jnp.zeros((BLOCK, LANES), F32)
    for k in range(n_pairs):
        high, low = split(of_all(k) * from_code)
        where_to = jnp.concatenate(
            [jnp.where(numbers[b : b + 1, :] == place, 1.0, 0.0).astype(BF16) for b in (2 * k, 2 * k + 1)], axis=0
        )
        both = mm(jnp.concatenate([where_to, where_to], axis=1), jnp.concatenate([high, low], axis=0))
        both = jnp.where(lane64 >= GROUP, both[GROUP:, :], both[:GROUP, :])
        by_q = [both[q * BLOCK : (q + 1) * BLOCK, :] for q in range(SIDE)]
        for piece in by_q:
            squares = squares + piece * piece
        high, low = split(halves(by_q))
        spec_high[k * 2 * BLOCK : (k + 1) * 2 * BLOCK, :] = high
        spec_low[k * 2 * BLOCK : (k + 1) * 2 * BLOCK, :] = low
    sums_ref[0] = squares
    for other in range(SECTIONS):

        @pl.when(section != other)
        def _():
            d = (other - section + SECTIONS) % SECTIONS
            remote(sums_ref.at[0], sums_ref.at[d], SEND_Z, z_recv, (replica, other)).start()

    col_load.wait()
    tall = SIDE * GROUP
    pieces = [col_tab[i * tall : (i + 1) * tall, :] for i in range(2 * BLOCK * GROUP // LANES)]
    col_high = jnp.concatenate(pieces[: len(pieces) // 2], axis=1)
    col_low = jnp.concatenate(pieces[len(pieces) // 2 :], axis=1)
    for s in range(OWNERS):
        part = slice(s * pairs * 2 * BLOCK, (s + 1) * pairs * 2 * BLOCK)
        cols = slice(s * width, (s + 1) * width)
        high, low = spec_high[part, :], spec_low[part, :]
        wide = mm(high, col_high) + mm(low, col_high) + mm(high, col_low)
        stacked = []
        for j in range(pairs):
            first = [wide[2 * j * BLOCK : (2 * j + 1) * BLOCK, a * LANES : (a + 1) * LANES] for a in range(BLOCK // 2)]
            second = [wide[(2 * j + 1) * BLOCK : (2 * j + 2) * BLOCK, a * LANES : (a + 1) * LANES] for a in range(BLOCK // 2)]
            by_i = []
            for a, b in zip(first, second):
                by_i.append(jnp.where(upper, pltpu.roll(b, GROUP, 1), a))
                by_i.append(jnp.where(upper, b, pltpu.roll(a, GROUP, 1)))
            stacked.append(jnp.concatenate(by_i, axis=0))
        high, low = split(jnp.concatenate(stacked, axis=1))
        total_high[:, cols] = high
        total_low[:, cols] = low
    for s in range(OWNERS):
        cols = slice(s * width, (s + 1) * width)
        high, low = total_high[:, cols], total_low[:, cols]
        total_ref[:, cols] = mm(left_inv_ip, jnp.concatenate([high, low, high], axis=0))

    received(sums_ref.at[1:SECTIONS], z_recv)

    n_y = (CHIPS_Y - 1) * ROWS_SENT // 2
    sent(wide_tiles.at[0:n_y], SEND_Y)
    sent(tiles.at[0:3], SEND_X)
    sent(tiles.at[0:4], SEND_CORE)
    sent(sums_ref.at[1:SECTIONS], SEND_Z)


def finish(entry_count, width, nm_ref, total_ref, sums_ref, nm_out, upd_out, upd, sem):
    stores = [pltpu.make_async_copy(nm_ref, nm_out, sem.at[0])]
    stores[0].start()
    squares = jnp.sum(sums_ref[...], axis=0)
    squares = jnp.sum(jnp.sum(squares, axis=0, keepdims=True), axis=1, keepdims=True)
    scale = lax.rsqrt(squares / entry_count + epsilon)
    for k in range(OWNERS // 2):
        for s in (2 * k, 2 * k + 1):
            upd[:, s * width : (s + 1) * width] = (total_ref[:, s * width : (s + 1) * width] * scale).astype(BF16)
        cols = slice(2 * k * width, 2 * (k + 1) * width)
        stores.append(pltpu.make_async_copy(upd.at[:, cols], upd_out.at[:, cols], sem.at[1 + k]))
        stores[-1].start()
    for copy in stores:
        copy.wait()


def per_device(gradients, momentum, keep_block):
    local_rows, columns = gradients.shape[1:]
    pairs = columns // (OWNERS * LANES)
    width = pairs * LANES
    tables = jnp.asarray(constant_tables())
    col_table = jnp.asarray(column_table())
    entry_count = float(local_rows * lax.axis_size("section") * columns)
    dma = pltpu.SemaphoreType.DMA
    new_momentum, total, sums = pl.pallas_call(
        functools.partial(kernel, pairs),
        out_shape=(
            pltpu.VMEM((local_rows, columns), F32),
            pltpu.VMEM((local_rows, columns), F32),
            pltpu.VMEM((SECTIONS, BLOCK, LANES), F32),
        ),
        in_specs=[pl.BlockSpec(memory_space=pltpu.HBM)] * 5,
        out_specs=(pl.BlockSpec(memory_space=pltpu.VMEM),) * 3,
        scratch_shapes=[
            pltpu.SMEM(keep_block.shape[1:], jnp.int32),
            pltpu.VMEM(keep_block.shape[1:], jnp.int32),
            pltpu.VMEM((local_rows, columns), BF16),
            pltpu.VMEM((local_rows, columns), F32),
            pltpu.VMEM(tables.shape, BF16),
            pltpu.VMEM(col_table.shape, BF16),
            pltpu.VMEM((OWNERS * pairs * BLOCK, LANES), F32),
            pltpu.VMEM((LANES, LANES), BF16),
            pltpu.VMEM((CHIPS_Y, CORES, CHIPS_X, ROWS_SENT, LANES), jnp.int16),
            pltpu.VMEM((CHIPS_Y * CORES * CHIPS_X * ROWS_SENT, LANES), F32),
            pltpu.VMEM((OWNERS * pairs * 2 * BLOCK, SIDE * GROUP), BF16),
            pltpu.VMEM((OWNERS * pairs * 2 * BLOCK, SIDE * GROUP), BF16),
            pltpu.VMEM((local_rows, columns), BF16),
            pltpu.VMEM((local_rows, columns), BF16),
            dma((6,)), dma((2,)), dma((4,)), dma((CHIPS_Y,)), dma((CHIPS_Y,)), dma((CHIPS_Y,)), dma,
        ],
        compiler_params=pltpu.CompilerParams(collective_id=0, has_side_effects=True, vmem_limit_bytes=56 << 20),
        name="kept_blocks_step",
    )(keep_block[0], gradients[0], momentum[0], tables, col_table)
    hbm = pl.BlockSpec(memory_space=pltpu.HBM)
    new_momentum, update = pl.pallas_call(
        functools.partial(finish, entry_count, width),
        out_shape=(
            jax.ShapeDtypeStruct((local_rows, columns), F32),
            jax.ShapeDtypeStruct((local_rows, columns), BF16),
        ),
        in_specs=[pl.BlockSpec(memory_space=pltpu.VMEM)] * 3,
        out_specs=(hbm, hbm),
        scratch_shapes=[pltpu.VMEM((local_rows, columns), BF16), dma((1 + OWNERS // 2,))],
        compiler_params=pltpu.CompilerParams(vmem_limit_bytes=32 << 20),
        name="scale_and_store",
    )(new_momentum, total, sums)
    return new_momentum[None], update


def solution(mesh):
    placed = (
        P("replica", "section", None),
        P("replica", "section", None),
        P("replica", "section", None),
    )
    return jax.shard_map(
        per_device,
        mesh=mesh,
        in_specs=placed,
        out_specs=(P("replica", "section", None), P("section", None)),
        check_vma=False,
    )
```

time: 38.6 us -> 33.5 us (0.87)
  Pallas kernels: 37.5 us -> 32.8 us
    pallas_call x1, Pallas kernels: 36.2 us -> 31.5 us  [per_device(): pl.pallas_call(functools.partial(kernel, pairs), out_shape=(pltpu.VMEM((l...]
where the time goes in v4:
time: 33.5 us; the launch traced here: 33.4 us
  Pallas kernels  32.8 us (98%)
  between operations  0.64 us (2%)
    pallas_call x1, Pallas kernels, per_device(): pl.pallas_call(functools.partial(kernel, pairs), out_shape=(pltpu.VMEM((l...  31.5 us
    pallas_call x1, Pallas kernels, per_device(): pl.pallas_call(functools.partial(finish, entry_count, width), out_shape=(...  1.31 us

profile of v4, /device:TPU:1, one launch (start us, length us, event | category | flops | bytes accessed | tf_op | source)
XLA Modules:
  0.0 33.4 jit_solution(4402104572280469373)
XLA Ops:
  0.6 31.5 %kept_blocks_step.1 = (f32[64,5120]{1,0:T(8,128)S(1)}, f32[64,5120]{1,0:T(8,128)S(1)}, f32[8,8,128]{2,1,0:T(8,128)S(1)}) custom-call(s32[1,80]{1,0:T(1,128)} %bitcast.6, bf16[64,5120]{1,0:T(8,128)(2,1)} %bitcast.5, f32[64,5120]{1,0:T(8,128)} %bitcast.4, bf16[1152,128]{1,0:T(8,128)(2,1)} %constant.4.clone.tab_ref, bf16[4096,128]{1,0:T(8,128)(2,1)} %constant.5.clone.col_ref), custom_call_target="tpu_custom_call" | custom-call | tf_op jit(solution)/shard_map/kept_blocks_step/pallas_call | solution.py:367
  32.1 1.3 %scale_and_store.1 = (f32[64,5120]{1,0:T(8,128)}, bf16[64,5120]{1,0:T(8,128)(2,1)}) custom-call(f32[64,5120]{1,0:T(8,128)S(1)} %get-tuple-element.7.nm_ref, f32[64,5120]{1,0:T(8,128)S(1)} %get-tuple-element.8.total_ref, f32[8,8,128]{2,1,0:T(8,128)S(1)} %get-tuple-element.9.sums_ref), custom_call_target="tpu_custom_call" | custom-call | tf_op jit(solution)/shard_map/scale_and_store/pallas_call | solution.py:397

commit v5 on v4

--- a/solution.py
+++ b/solution.py
@@ -17,7 +17,7 @@
 OWNERS = CHIPS_X * CORES
 MESH = pl.DeviceIdType.MESH
 ROWS_SENT = 48
-TOP = 32000.0
+TOP_BITS = 15
 F32, BF16 = jnp.float32, jnp.bfloat16
 
 momentum_decay = 0.9
@@ -75,7 +75,7 @@
 
 def kernel(
     pairs, kb_hbm, g_ref, m_ref, tab_ref, col_ref, nm_ref, total_ref, sums_ref,
-    kb_ref, kb_row, g_buf, m_buf, tab, col_tab, masked, fold, tiles, wide_tiles, spec_high, spec_low, total_high, total_low,
+    kb_ref, kb_row, g_buf, m_buf, tab, col_tab, masked, fold, tiles, wide_tiles, spectra, spec_high, spec_low, wide_cols, total_high, total_low,
     load_sem, kb_sem, send_sem, y_recv, x_recv, core_recv, z_recv,
 ):
     width = pairs * LANES
@@ -114,7 +114,6 @@
             tab_load.start()
 
     col_load = pltpu.make_async_copy(col_ref, col_tab, load_sem.at[5])
-    col_load.start()
 
     barrier = pltpu.get_barrier_semaphore()
     everyone = (
@@ -174,6 +173,8 @@
                 picked = jnp.where(p_of == p, rows[p * BLOCK : (p + 1) * BLOCK, j * LANES : (j + 1) * LANES], picked)
             chosen.append(picked)
 
+    col_load.start()
+
     high, low = split(jnp.concatenate(chosen, axis=0))
     spectrum = mm(jnp.concatenate([high, low, high], axis=1), right_fwd)
     for s in range(OWNERS):
@@ -198,7 +199,7 @@
         largest = jnp.maximum(largest, jnp.abs(line))
     largest = jnp.max(jnp.max(largest, axis=0, keepdims=True), axis=1, keepdims=True)
     exponent = jnp.ceil(jnp.log2(jnp.maximum(largest, 1e-30)) + 0.01)
-    to_code = TOP * jnp.exp2(-exponent)
+    to_code = jnp.exp2(TOP_BITS - exponent)
     coded = [jnp.round(line * to_code) for line in lines]
     coded.append(jnp.where(row8 == 0, numbers, jnp.where(row8 == 1, exponent, 0.0)))
     coded = jnp.concatenate(coded, axis=0).astype(jnp.int32).astype(jnp.int16)
@@ -243,7 +244,7 @@
         high, low = split(jnp.concatenate(placed, axis=1))
         nm_ref[:, cols] = nm_ref[:, cols] - mm(left_inv, jnp.concatenate([high, low, high], axis=0))
 
-    lag = 4
+    lag = 7
     for k in range(CHIPS_Y + lag):
         if k < CHIPS_Y:
             row = row_order[k]
@@ -272,30 +273,34 @@
     def of_all(line):
         return wide_tiles[pl.ds(line, n_replica, stride=ROWS_SENT), :]
 
-    row_n = lax.broadcasted_iota(jnp.int32, (2 * n_pairs, LANES), 0)
-    lane_n = lax.broadcasted_iota(jnp.int32, (2 * n_pairs, LANES), 1)
-    pick = jnp.where(row_n == lane_n, 1.0, 0.0).astype(BF16)
-    numbers = lax.dot_general(
-        pick, of_all(n_pairs).astype(BF16), (((1,), (1,)), ((), ())), preferred_element_type=F32
+    def across(lines, rows):
+        return lax.dot_general(rows, lines.astype(BF16), (((1,), (1,)), ((), ())), preferred_element_type=F32)
+
+    row_n = lax.broadcasted_iota(jnp.int32, (n_pairs, LANES), 0)
+    lane_n = lax.broadcasted_iota(jnp.int32, (n_pairs, LANES), 1)
+    of_numbers = of_all(n_pairs)
+    numbers = jnp.concatenate(
+        [across(of_numbers, jnp.where(lane_n == 2 * row_n + h, 1.0, 0.0).astype(BF16)) for h in range(2)], axis=1
     )
-    from_code = jnp.exp2(of_all(n_pairs + 1)) * (1.0 / TOP)
-    row_place = lax.broadcasted_iota(jnp.int32, (GROUP, n_replica), 0)
+    exponents = across(of_all(n_pairs + 1), jnp.where(lane8 == 0, 1.0, 0.0).astype(BF16))[0:1, :]
+    from_code = jnp.exp2(jnp.concatenate([exponents, exponents], axis=1) - TOP_BITS)
+    row_place = lax.broadcasted_iota(jnp.int32, (GROUP, LANES), 0)
     place = ((row_place % BLOCK) * SIDE + row_place // BLOCK).astype(F32)
     lane64 = lax.broadcasted_iota(jnp.int32, (GROUP, LANES), 1)
+    of_first = jnp.where(lane64 < GROUP, 1.0, 0.0).astype(BF16)
+    of_second = jnp.where(lane64 < GROUP, 0.0, 1.0).astype(BF16)
     squares = jnp.zeros((BLOCK, LANES), F32)
     for k in range(n_pairs):
-        high, low = split(of_all(k) * from_code)
-        where_to = jnp.concatenate(
-            [jnp.where(numbers[b : b + 1, :] == place, 1.0, 0.0).astype(BF16) for b in (2 * k, 2 * k + 1)], axis=0
+        high, low = split(of_all(k))
+        where_to = jnp.where(numbers[k : k + 1, :] == place, from_code, 0.0).astype(BF16)
+        both = mm(
+            jnp.concatenate([where_to, where_to], axis=1),
+            jnp.concatenate([high * of_first, high * of_second, low * of_first, low * of_second], axis=0),
         )
-        both = mm(jnp.concatenate([where_to, where_to], axis=1), jnp.concatenate([high, low], axis=0))
-        both = jnp.where(lane64 >= GROUP, both[GROUP:, :], both[:GROUP, :])
-        by_q = [both[q * BLOCK : (q + 1) * BLOCK, :] for q in range(SIDE)]
-        for piece in by_q:
+        spectra[k * GROUP : (k + 1) * GROUP, :] = both
+        for q in range(SIDE):
+            piece = both[q * BLOCK : (q + 1) * BLOCK, :]
             squares = squares + piece * piece
-        high, low = split(halves(by_q))
-        spec_high[k * 2 * BLOCK : (k + 1) * 2 * BLOCK, :] = high
-        spec_low[k * 2 * BLOCK : (k + 1) * 2 * BLOCK, :] = low
     sums_ref[0] = squares
     for other in range(SECTIONS):
 
@@ -309,23 +314,30 @@
     pieces = [col_tab[i * tall : (i + 1) * tall, :] for i in range(2 * BLOCK * GROUP // LANES)]
     col_high = jnp.concatenate(pieces[: len(pieces) // 2], axis=1)
     col_low = jnp.concatenate(pieces[len(pieces) // 2 :], axis=1)
-    for s in range(OWNERS):
-        part = slice(s * pairs * 2 * BLOCK, (s + 1) * pairs * 2 * BLOCK)
-        cols = slice(s * width, (s + 1) * width)
-        high, low = spec_high[part, :], spec_low[part, :]
-        wide = mm(high, col_high) + mm(low, col_high) + mm(high, col_low)
-        stacked = []
-        for j in range(pairs):
-            first = [wide[2 * j * BLOCK : (2 * j + 1) * BLOCK, a * LANES : (a + 1) * LANES] for a in range(BLOCK // 2)]
-            second = [wide[(2 * j + 1) * BLOCK : (2 * j + 2) * BLOCK, a * LANES : (a + 1) * LANES] for a in range(BLOCK // 2)]
+    for k in range(n_pairs):
+        by_q = [spectra[k * GROUP + q * BLOCK : k * GROUP + (q + 1) * BLOCK, :] for q in range(SIDE)]
+        high, low = split(halves(by_q))
+        spec_high[k * 2 * BLOCK : (k + 1) * 2 * BLOCK, :] = high
+        spec_low[k * 2 * BLOCK : (k + 1) * 2 * BLOCK, :] = low
+    for side in range(2):
+        half_cols = slice(side * 2 * LANES, (side + 1) * 2 * LANES)
+        wide_cols[...] = (
+            mm(spec_high[...], col_high[:, half_cols])
+            + mm(spec_low[...], col_high[:, half_cols])
+            + mm(spec_high[...], col_low[:, half_cols])
+        )
+        for k in range(n_pairs):
             by_i = []
-            for a, b in zip(first, second):
-                by_i.append(jnp.where(upper, pltpu.roll(b, GROUP, 1), a))
-                by_i.append(jnp.where(upper, b, pltpu.roll(a, GROUP, 1)))
-            stacked.append(jnp.concatenate(by_i, axis=0))
-        high, low = split(jnp.concatenate(stacked, axis=1))
-        total_high[:, cols] = high
-        total_low[:, cols] = low
+            for a in range(2):
+                lanes = slice(a * LANES, (a + 1) * LANES)
+                first = wide_cols[2 * k * BLOCK : (2 * k + 1) * BLOCK, lanes]
+                second = wide_cols[(2 * k + 1) * BLOCK : (2 * k + 2) * BLOCK, lanes]
+                by_i.append(jnp.where(upper, pltpu.roll(second, GROUP, 1), first))
+                by_i.append(jnp.where(upper, second, pltpu.roll(first, GROUP, 1)))
+            high, low = split(jnp.concatenate(by_i, axis=0))
+            rows = slice(side * GROUP // 2, (side + 1) * GROUP // 2)
+            total_high[rows, k * LANES : (k + 1) * LANES] = high
+            total_low[rows, k * LANES : (k + 1) * LANES] = low
     for s in range(OWNERS):
         cols = slice(s * width, (s + 1) * width)
         high, low = total_high[:, cols], total_low[:, cols]
@@ -384,8 +396,10 @@
             pltpu.VMEM((LANES, LANES), BF16),
             pltpu.VMEM((CHIPS_Y, CORES, CHIPS_X, ROWS_SENT, LANES), jnp.int16),
             pltpu.VMEM((CHIPS_Y * CORES * CHIPS_X * ROWS_SENT, LANES), F32),
+            pltpu.VMEM((OWNERS * pairs * GROUP, LANES), F32),
             pltpu.VMEM((OWNERS * pairs * 2 * BLOCK, SIDE * GROUP), BF16),
             pltpu.VMEM((OWNERS * pairs * 2 * BLOCK, SIDE * GROUP), BF16),
+            pltpu.VMEM((OWNERS * pairs * 2 * BLOCK, 2 * LANES), F32),
             pltpu.VMEM((local_rows, columns), BF16),
             pltpu.VMEM((local_rows, columns), BF16),
             dma((6,)), dma((2,)), dma((4,)), dma((CHIPS_Y,)), dma((CHIPS_Y,)), dma((CHIPS_Y,)), dma,

time: 33.5 us -> 32.1 us (0.958)
  Pallas kernels: 32.8 us -> 31.3 us
    pallas_call x1, Pallas kernels: 31.5 us -> 30 us  [per_device(): pl.pallas_call(functools.partial(kernel, pairs), out_shape=(pltpu.VMEM((l...]
where the time goes in v5:
time: 32.1 us; the launch traced here: 31.9 us
  Pallas kernels  31.3 us (98%)
  between operations  0.64 us (2%)
    pallas_call x1, Pallas kernels, per_device(): pl.pallas_call(functools.partial(kernel, pairs), out_shape=(pltpu.VMEM((l...  30 us
    pallas_call x1, Pallas kernels, per_device(): pl.pallas_call(functools.partial(finish, entry_count, width), out_shape=(...  1.31 us

profile of v5, /device:TPU:1, one launch (start us, length us, event | category | flops | bytes accessed | tf_op | source)
XLA Modules:
  0.0 31.9 jit_solution(10862820022097518459)
XLA Ops:
  0.6 30.0 %kept_blocks_step.1 = (f32[64,5120]{1,0:T(8,128)S(1)}, f32[64,5120]{1,0:T(8,128)S(1)}, f32[8,8,128]{2,1,0:T(8,128)S(1)}) custom-call(s32[1,80]{1,0:T(1,128)} %bitcast.6, bf16[64,5120]{1,0:T(8,128)(2,1)} %bitcast.5, f32[64,5120]{1,0:T(8,128)} %bitcast.4, bf16[1152,128]{1,0:T(8,128)(2,1)} %constant.4.clone.tab_ref, bf16[4096,128]{1,0:T(8,128)(2,1)} %constant.5.clone.col_ref), custom_call_target="tpu_custom_call" | custom-call | tf_op jit(solution)/shard_map/kept_blocks_step/pallas_call | solution.py:379
  30.6 1.3 %scale_and_store.1 = (f32[64,5120]{1,0:T(8,128)}, bf16[64,5120]{1,0:T(8,128)(2,1)}) custom-call(f32[64,5120]{1,0:T(8,128)S(1)} %get-tuple-element.7.nm_ref, f32[64,5120]{1,0:T(8,128)S(1)} %get-tuple-element.8.total_ref, f32[8,8,128]{2,1,0:T(8,128)S(1)} %get-tuple-element.9.sums_ref), custom_call_target="tpu_custom_call" | custom-call | tf_op jit(solution)/shard_map/scale_and_store/pallas_call | solution.py:411

commit v6 on v5

--- a/solution.py
+++ b/solution.py
@@ -93,6 +93,7 @@
     group_y = sorted(range(1, CHIPS_Y), key=lambda d: -min(d, CHIPS_Y - d))
     group_x = (2, 1, 3)
     row_order = (0, 2, 3, 1, 6, 7, 5, 4)
+    grouped = 4
 
     half = OWNERS // 2 * width
     loads = []
@@ -177,10 +178,13 @@
 
     high, low = split(jnp.concatenate(chosen, axis=0))
     spectrum = mm(jnp.concatenate([high, low, high], axis=1), right_fwd)
+    largest = jnp.zeros((BLOCK, LANES), F32)
     for s in range(OWNERS):
         for j in range(pairs):
             row = (s * pairs + j) * BLOCK
-            masked[row : row + BLOCK, :] = jnp.where(q_lanes(s, j) == lane_q, spectrum[row : row + BLOCK, :], 0.0)
+            kept = jnp.where(q_lanes(s, j) == lane_q, spectrum[row : row + BLOCK, :], 0.0)
+            masked[row : row + BLOCK, :] = kept
+            largest = jnp.maximum(largest, jnp.abs(kept))
 
     kept_high, kept_low = split(masked[...])
     folded = mm(kept_high, fold[...]) + mm(kept_low, fold[...])
@@ -194,9 +198,6 @@
         else:
             lines[-1] = jnp.where(row8 == k % BLOCK, piece, lines[-1])
 
-    largest = jnp.abs(lines[0])
-    for line in lines[1:]:
-        largest = jnp.maximum(largest, jnp.abs(line))
     largest = jnp.max(jnp.max(largest, axis=0, keepdims=True), axis=1, keepdims=True)
     exponent = jnp.ceil(jnp.log2(jnp.maximum(largest, 1e-30)) + 0.01)
     to_code = jnp.exp2(TOP_BITS - exponent)
@@ -221,12 +222,13 @@
         remote(ref, ref, which, z_recv, peer(dc=1)).wait_send()
 
     def along_x(row):
+        mark = jnp.maximum(row - grouped + 1, 0)
         for d in group_x:
-            remote(tiles.at[row, core, 0], tiles.at[row, core, CHIPS_X - d], SEND_X, x_recv.at[row], peer(dx=d)).start()
-
-    def to_core(row):
-        received(tiles.at[row, core, 1:CHIPS_X], x_recv.at[row])
-        remote(tiles.at[row, core], tiles.at[row, core], SEND_CORE, core_recv.at[row], peer(dc=1)).start()
+            remote(tiles.at[row, core, 0], tiles.at[row, core, CHIPS_X - d], SEND_X, x_recv.at[mark], peer(dx=d)).start()
+
+    def to_core(rows, mark):
+        received(tiles.at[rows, core, 1:CHIPS_X], x_recv.at[mark])
+        remote(tiles.at[rows, core], tiles.at[rows, core], SEND_CORE, core_recv.at[mark], peer(dc=1)).start()
 
     for d in group_y:
         remote(tiles.at[y, core, 0], tiles.at[y, core, 0], SEND_Y, y_recv.at[y], peer(dy=d)).start()
@@ -244,22 +246,23 @@
         high, low = split(jnp.concatenate(placed, axis=1))
         nm_ref[:, cols] = nm_ref[:, cols] - mm(left_inv, jnp.concatenate([high, low, high], axis=0))
 
-    lag = 7
-    for k in range(CHIPS_Y + lag):
-        if k < CHIPS_Y:
-            row = row_order[k]
-
-            @pl.when(y != row)
-            def _():
-                received(tiles.at[row, core, 0], y_recv.at[row])
-                along_x(row)
-
-        if k >= lag:
-            to_core(row_order[k - lag])
+    for row in row_order:
+
+        @pl.when(y != row)
+        def _():
+            received(tiles.at[row, core, 0], y_recv.at[row])
+            along_x(row)
+
+    late_rows = row_order[grouped:]
+    to_core(slice(0, grouped), 0)
+    for row in late_rows:
+        to_core(row, row - grouped + 1)
     n_replica = CHIPS_Y * CORES * CHIPS_X
     of_row = CORES * CHIPS_X * ROWS_SENT
-    for row in row_order:
-        received(tiles.at[row, 1 - core], core_recv.at[row])
+    received(tiles.at[0:grouped, 1 - core], core_recv.at[0])
+    for row in tuple(range(grouped)) + late_rows:
+        if row >= grouped:
+            received(tiles.at[row, 1 - core], core_recv.at[row - grouped + 1])
         values = tiles[row].reshape(of_row, LANES).astype(jnp.int32).astype(F32)
         wide_tiles[row * of_row : (row + 1) * of_row, :] = values
 
@@ -395,14 +398,14 @@
             pltpu.VMEM((OWNERS * pairs * BLOCK, LANES), F32),
             pltpu.VMEM((LANES, LANES), BF16),
             pltpu.VMEM((CHIPS_Y, CORES, CHIPS_X, ROWS_SENT, LANES), jnp.int16),
-            pltpu.VMEM((CHIPS_Y * CORES * CHIPS_X * ROWS_SENT, LANES), F32),
+            pltpu.VMEM(((CHIPS_Y * CORES * CHIPS_X + 1) * ROWS_SENT, LANES), F32),
             pltpu.VMEM((OWNERS * pairs * GROUP, LANES), F32),
             pltpu.VMEM((OWNERS * pairs * 2 * BLOCK, SIDE * GROUP), BF16),
             pltpu.VMEM((OWNERS * pairs * 2 * BLOCK, SIDE * GROUP), BF16),
             pltpu.VMEM((OWNERS * pairs * 2 * BLOCK, 2 * LANES), F32),
             pltpu.VMEM((local_rows, columns), BF16),
             pltpu.VMEM((local_rows, columns), BF16),
-            dma((6,)), dma((2,)), dma((4,)), dma((CHIPS_Y,)), dma((CHIPS_Y,)), dma((CHIPS_Y,)), dma,
+            dma((6,)), dma((2,)), dma((4,)), dma((CHIPS_Y,)), dma((5,)), dma((5,)), dma,
         ],
         compiler_params=pltpu.CompilerParams(collective_id=0, has_side_effects=True, vmem_limit_bytes=56 << 20),
         name="kept_blocks_step",

time: 32.1 us -> 32 us (level)
  no operation moved by 1% of the time
where the time goes in v6:
time: 32 us; the launch traced here: 31.8 us
  Pallas kernels  31.2 us (98%)
  between operations  0.64 us (2%)
    pallas_call x1, Pallas kernels, per_device(): pl.pallas_call(functools.partial(kernel, pairs), out_shape=(pltpu.VMEM((l...  29.9 us
    pallas_call x1, Pallas kernels, per_device(): pl.pallas_call(functools.partial(finish, entry_count, width), out_shape=(...  1.31 us

profile of v6, /device:TPU:1, one launch (start us, length us, event | category | flops | bytes accessed | tf_op | source)
XLA Modules:
  0.0 31.8 jit_solution(6453482940906920066)
XLA Ops:
  0.6 29.9 %kept_blocks_step.1 = (f32[64,5120]{1,0:T(8,128)S(1)}, f32[64,5120]{1,0:T(8,128)S(1)}, f32[8,8,128]{2,1,0:T(8,128)S(1)}) custom-call(s32[1,80]{1,0:T(1,128)} %bitcast.6, bf16[64,5120]{1,0:T(8,128)(2,1)} %bitcast.5, f32[64,5120]{1,0:T(8,128)} %bitcast.4, bf16[1152,128]{1,0:T(8,128)(2,1)} %constant.4.clone.tab_ref, bf16[4096,128]{1,0:T(8,128)(2,1)} %constant.5.clone.col_ref), custom_call_target="tpu_custom_call" | custom-call | tf_op jit(solution)/shard_map/kept_blocks_step/pallas_call | solution.py:382
  30.5 1.3 %scale_and_store.1 = (f32[64,5120]{1,0:T(8,128)}, bf16[64,5120]{1,0:T(8,128)(2,1)}) custom-call(f32[64,5120]{1,0:T(8,128)S(1)} %get-tuple-element.7.nm_ref, f32[64,5120]{1,0:T(8,128)S(1)} %get-tuple-element.8.total_ref, f32[8,8,128]{2,1,0:T(8,128)S(1)} %get-tuple-element.9.sums_ref), custom_call_target="tpu_custom_call" | custom-call | tf_op jit(solution)/shard_map/scale_and_store/pallas_call | solution.py:414

commit v7 on v6

--- a/solution.py
+++ b/solution.py
@@ -93,6 +93,7 @@
     group_y = sorted(range(1, CHIPS_Y), key=lambda d: -min(d, CHIPS_Y - d))
     group_x = (2, 1, 3)
     row_order = (0, 2, 3, 1, 6, 7, 5, 4)
+    direct = (4, 5)
     grouped = 4
 
     half = OWNERS // 2 * width
@@ -122,6 +123,7 @@
         + [peer(dy=d) for d in group_y]
         + [peer(dz=d) for d in range(1, SECTIONS)]
         + [peer(dc=1)]
+        + [peer(dx=d, dc=1) for d in group_x]
     )
     for other in everyone:
         pl.semaphore_signal(barrier, inc=1, device_id=other, device_id_type=MESH)
@@ -224,11 +226,25 @@
     def along_x(row):
         mark = jnp.maximum(row - grouped + 1, 0)
         for d in group_x:
-            remote(tiles.at[row, core, 0], tiles.at[row, core, CHIPS_X - d], SEND_X, x_recv.at[mark], peer(dx=d)).start()
+            there = tiles.at[row, core, CHIPS_X - d]
+            remote(tiles.at[row, core, 0], there, SEND_X, x_recv.at[mark], peer(dx=d)).start()
+
+        def to_both():
+            for d in group_x:
+                there = tiles.at[row, core, CHIPS_X - d]
+                remote(tiles.at[row, core, 0], there, SEND_CORE, core_recv.at[mark], peer(dx=d, dc=1)).start()
+            remote(tiles.at[row, core, 0], tiles.at[row, core, 0], SEND_CORE, core_recv.at[mark], peer(dc=1)).start()
+
+        if isinstance(row, int):
+            if row in direct:
+                to_both()
+        else:
+            pl.when(sum((row == r).astype(jnp.int32) for r in direct) > 0)(to_both)
 
     def to_core(rows, mark):
         received(tiles.at[rows, core, 1:CHIPS_X], x_recv.at[mark])
-        remote(tiles.at[rows, core], tiles.at[rows, core], SEND_CORE, core_recv.at[mark], peer(dc=1)).start()
+        if rows not in direct:
+            remote(tiles.at[rows, core], tiles.at[rows, core], SEND_CORE, core_recv.at[mark], peer(dc=1)).start()
 
     for d in group_y:
         remote(tiles.at[y, core, 0], tiles.at[y, core, 0], SEND_Y, y_recv.at[y], peer(dy=d)).start()

time: 32 us -> 31.6 us (0.988)
  Pallas kernels: 31.2 us -> 30.8 us
    pallas_call x1, Pallas kernels: 29.9 us -> 29.5 us  [per_device(): pl.pallas_call(functools.partial(kernel, pairs), out_shape=(pltpu.VMEM((l...]
where the time goes in v7:
time: 31.6 us; the launch traced here: 31.5 us
  Pallas kernels  30.8 us (97%)
  between operations  0.64 us (2%)
    pallas_call x1, Pallas kernels, per_device(): pl.pallas_call(functools.partial(kernel, pairs), out_shape=(pltpu.VMEM((l...  29.5 us
    pallas_call x1, Pallas kernels, per_device(): pl.pallas_call(functools.partial(finish, entry_count, width), out_shape=(...  1.31 us

profile of v7, /device:TPU:1, one launch (start us, length us, event | category | flops | bytes accessed | tf_op | source)
XLA Modules:
  0.0 31.5 jit_solution(12013741597826267932)
XLA Ops:
  0.6 29.5 %kept_blocks_step.1 = (f32[64,5120]{1,0:T(8,128)S(1)}, f32[64,5120]{1,0:T(8,128)S(1)}, f32[8,8,128]{2,1,0:T(8,128)S(1)}) custom-call(s32[1,80]{1,0:T(1,128)} %bitcast.6, bf16[64,5120]{1,0:T(8,128)(2,1)} %bitcast.5, f32[64,5120]{1,0:T(8,128)} %bitcast.4, bf16[1152,128]{1,0:T(8,128)(2,1)} %constant.4.clone.tab_ref, bf16[4096,128]{1,0:T(8,128)(2,1)} %constant.5.clone.col_ref), custom_call_target="tpu_custom_call" | custom-call | tf_op jit(solution)/shard_map/kept_blocks_step/pallas_call | solution.py:398
  30.1 1.3 %scale_and_store.1 = (f32[64,5120]{1,0:T(8,128)}, bf16[64,5120]{1,0:T(8,128)(2,1)}) custom-call(f32[64,5120]{1,0:T(8,128)S(1)} %get-tuple-element.7.nm_ref, f32[64,5120]{1,0:T(8,128)S(1)} %get-tuple-element.8.total_ref, f32[8,8,128]{2,1,0:T(8,128)S(1)} %get-tuple-element.9.sums_ref), custom_call_target="tpu_custom_call" | custom-call | tf_op jit(solution)/shard_map/scale_and_store/pallas_call | solution.py:430

commit v8 on v6

--- a/solution.py
+++ b/solution.py
@@ -93,6 +93,7 @@
     group_y = sorted(range(1, CHIPS_Y), key=lambda d: -min(d, CHIPS_Y - d))
     group_x = (2, 1, 3)
     row_order = (0, 2, 3, 1, 6, 7, 5, 4)
+    direct = (4, 5)
     grouped = 4
 
     half = OWNERS // 2 * width
@@ -122,6 +123,7 @@
         + [peer(dy=d) for d in group_y]
         + [peer(dz=d) for d in range(1, SECTIONS)]
         + [peer(dc=1)]
+        + [peer(dx=d, dc=1) for d in group_x]
     )
     for other in everyone:
         pl.semaphore_signal(barrier, inc=1, device_id=other, device_id_type=MESH)
@@ -223,12 +225,38 @@
 
     def along_x(row):
         mark = jnp.maximum(row - grouped + 1, 0)
+
+        def to_same(d):
+            there = tiles.at[row, core, CHIPS_X - d]
+            remote(tiles.at[row, core, 0], there, SEND_X, x_recv.at[mark], peer(dx=d)).start()
+
+        def to_other(d):
+            there = tiles.at[row, core, CHIPS_X - d]
+            remote(tiles.at[row, core, 0], there, SEND_CORE, core_recv.at[mark], peer(dx=d, dc=1)).start()
+
+        def to_partner():
+            remote(tiles.at[row, core, 0], tiles.at[row, core, 0], SEND_CORE, core_recv.at[mark], peer(dc=1)).start()
+
+        if isinstance(row, int) and row in direct:
+            for d in group_x:
+                to_other(d)
+                to_same(d)
+            to_partner()
+            return
         for d in group_x:
-            remote(tiles.at[row, core, 0], tiles.at[row, core, CHIPS_X - d], SEND_X, x_recv.at[mark], peer(dx=d)).start()
+            to_same(d)
+        if not isinstance(row, int):
+
+            @pl.when(sum((row == r).astype(jnp.int32) for r in direct) > 0)
+            def _():
+                for d in group_x:
+                    to_other(d)
+                to_partner()
 
     def to_core(rows, mark):
         received(tiles.at[rows, core, 1:CHIPS_X], x_recv.at[mark])
-        remote(tiles.at[rows, core], tiles.at[rows, core], SEND_CORE, core_recv.at[mark], peer(dc=1)).start()
+        if rows not in direct:
+            remote(tiles.at[rows, core], tiles.at[rows, core], SEND_CORE, core_recv.at[mark], peer(dc=1)).start()
 
     for d in group_y:
         remote(tiles.at[y, core, 0], tiles.at[y, core, 0], SEND_Y, y_recv.at[y], peer(dy=d)).start()

time: 32 us -> 31.6 us (0.988)
  Pallas kernels: 31.2 us -> 30.8 us
    pallas_call x1, Pallas kernels: 29.9 us -> 29.5 us  [per_device(): pl.pallas_call(functools.partial(kernel, pairs), out_shape=(pltpu.VMEM((l...]
where the time goes in v8:
time: 31.6 us; the launch traced here: 31.5 us
  Pallas kernels  30.8 us (97%)
  between operations  0.64 us (2%)
    pallas_call x1, Pallas kernels, per_device(): pl.pallas_call(functools.partial(kernel, pairs), out_shape=(pltpu.VMEM((l...  29.5 us
    pallas_call x1, Pallas kernels, per_device(): pl.pallas_call(functools.partial(finish, entry_count, width), out_shape=(...  1.31 us

profile of v8, /device:TPU:1, one launch (start us, length us, event | category | flops | bytes accessed | tf_op | source)
XLA Modules:
  0.0 31.5 jit_solution(7148291306504179638)
XLA Ops:
  0.6 29.5 %kept_blocks_step.1 = (f32[64,5120]{1,0:T(8,128)S(1)}, f32[64,5120]{1,0:T(8,128)S(1)}, f32[8,8,128]{2,1,0:T(8,128)S(1)}) custom-call(s32[1,80]{1,0:T(1,128)} %bitcast.6, bf16[64,5120]{1,0:T(8,128)(2,1)} %bitcast.5, f32[64,5120]{1,0:T(8,128)} %bitcast.4, bf16[1152,128]{1,0:T(8,128)(2,1)} %constant.4.clone.tab_ref, bf16[4096,128]{1,0:T(8,128)(2,1)} %constant.5.clone.col_ref), custom_call_target="tpu_custom_call" | custom-call | tf_op jit(solution)/shard_map/kept_blocks_step/pallas_call | solution.py:410
  30.2 1.3 %scale_and_store.1 = (f32[64,5120]{1,0:T(8,128)}, bf16[64,5120]{1,0:T(8,128)(2,1)}) custom-call(f32[64,5120]{1,0:T(8,128)S(1)} %get-tuple-element.7.nm_ref, f32[64,5120]{1,0:T(8,128)S(1)} %get-tuple-element.8.total_ref, f32[8,8,128]{2,1,0:T(8,128)S(1)} %get-tuple-element.9.sums_ref), custom_call_target="tpu_custom_call" | custom-call | tf_op jit(solution)/shard_map/scale_and_store/pallas_call | solution.py:442
